TPU v7x, 128 devices: a whole 4x4x4 slice. The times are simulated.
128 devices in a mesh: bin: 16 (over x, y_hi, core), dist: 8 (over z, y_lo).
Axes of the slice: x: 4, y: 4 (y_hi: 2, y_lo: 2; y = y_hi * 2 + y_lo), z: 4, core: 2. Of those that a mesh axis runs over, the one named last changes fastest.
Arguments:
- wavefuncs: bfloat16 [1536, 512], P('bin', 'dist'), may hold values from -6 to 6
- kernel: bfloat16 [512, 512], P(None, 'dist'), may hold values from -0.25 to 0.25
- labels: int32 [1536], P('bin'), may hold values from 0 to 7
- row_tiles: int32 [1024], P('bin'), may hold values from 0 to 2
- col_tiles: int32 [1024], P('bin'), may hold values from 0 to 47
- owners: int32 [1024, 1], P('bin'), may hold values from 0 to 15; in each aligned block of 64 rows (0 to 63, 64 to 127, ...) at most 8 rows name the same one
Outputs:
- owned_tiles: bfloat16 [2048, 512, 1024], P('bin', 'dist')
Inputs may be any that keep to these rules, and one draw needn't show every extreme that they name: `owners`: among the 64 entries of one sender no owner appears more than 8 times, and some owner appears exactly 8 times.
All inputs are finite; a program needn't handle non-finite values.
Results may differ from a plain program's by a relative error of at most 0.005.
Values may be sent and summed in bfloat16 or wider, within the bound.
A program may use at most 128 MiB of HBM per device.

v0:
```python
import jax
import jax.numpy as jnp
from jax import lax
from jax.sharding import PartitionSpec as P

R = 512
TB = 32
LMAX = 8
BIN_DEV = 96
SEL = 64


def angular(left_l, right_l):
    left_f = left_l.astype(jnp.float32)[..., :, None]
    right_f = right_l.astype(jnp.float32)[..., None, :]
    return jnp.sqrt((2.0 * left_f + 1.0) * (2.0 * right_f + 1.0)) / (
        LMAX * (1.0 + jnp.abs(left_f - right_f))
    )


def tile_forms(row_wave, col_wave, row_label, col_label, kernel):
    product = jnp.einsum(
        "kar,kbr->krab", row_wave.astype(jnp.float32), col_wave.astype(jnp.float32)
    )
    pair_bf = (product * angular(row_label, col_label)[:, None]).astype(jnp.bfloat16)
    pair_bf = pair_bf.reshape(pair_bf.shape[0], pair_bf.shape[1], -1)
    return jnp.einsum("rd,krq->kdq", kernel, pair_bf, preferred_element_type=jnp.float32).astype(
        jnp.bfloat16
    )


def blockwise(tile_wave, tile_label, row_index, col_index, kernel):

    def block_fn(pieces):
        row_piece, col_piece = pieces
        return tile_forms(
            tile_wave[row_piece],
            tile_wave[col_piece],
            tile_label[row_piece],
            tile_label[col_piece],
            kernel,
        )

    tile_out = lax.map(block_fn, (row_index.reshape(-1, 8), col_index.reshape(-1, 8)))
    return tile_out.reshape(row_index.shape[0], kernel.shape[1], TB * TB)


def per_device(wavefuncs, kernel, labels, row_tiles, col_tiles, owners):
    group_count = lax.axis_size("bin")
    own_index = lax.axis_index("bin")
    blocks_own = BIN_DEV // TB
    capacity = 2 * SEL // group_count
    dist_local = kernel.shape[1]
    whole_wave = lax.all_gather(wavefuncs, "dist", axis=1, tiled=True)
    label_bf = labels.astype(jnp.float32).astype(jnp.bfloat16)
    owner_list = owners[:, 0]
    all_wave, all_label = (
        lax.all_gather(whole_wave, "bin", axis=0, tiled=True),
        lax.all_gather(label_bf, "bin", axis=0, tiled=True),
    )
    row_global = row_tiles + own_index * blocks_own
    buffer = blockwise(
        all_wave.reshape(-1, TB, R), all_label.reshape(-1, TB), row_global, col_tiles, kernel
    )
    onehot = (owner_list[:, None] == jnp.arange(group_count, dtype=jnp.int32)[None, :]).astype(
        jnp.int32
    )
    slot_rank = jnp.sum((jnp.cumsum(onehot, axis=0) - onehot) * onehot, axis=1)
    target_row = owner_list * capacity + slot_rank
    outbox = (
        jnp.zeros((group_count * capacity, dist_local, TB * TB), jnp.bfloat16)
        .at[target_row]
        .set(buffer)
    )
    result = lax.all_to_all(outbox, "bin", split_axis=0, concat_axis=0, tiled=True)
    return result


def solution(mesh):
    return jax.shard_map(
        per_device,
        mesh=mesh,
        in_specs=(P("bin", "dist"), P(None, "dist"), P("bin"), P("bin"), P("bin"), P("bin", None)),
        out_specs=P("bin", "dist", None),
        check_vma=False,
    )
```

profile of v0, /device:TPU:1, one launch (start us, length us, event | category | flops | bytes accessed | tf_op | source)
XLA Modules:
  0.0 405.1 jit_solution(8569482135128518405)
XLA Ops:
  6.5 24.8 %all_gather.9 = bf16[96,512]{0,1:T(8,128)(2,1)S(1)} all-gather(bf16[96,64]{0,1:T(8,128)(2,1)} %param.8), channel_id=1, replica_groups=mesh['bin'=16,'dist'=8] {'dist'}, dimensions={1}, use_global_device_ids=true | all-gather | bytes 110592 | tf_op jit(solution)/shard_map/all_gather | solution.py:54
  36.3 39.3 %all-reduce = bf16[1536]{0:T(1024)(128)(2,1)S(1)} all-reduce(bf16[1536]{0:T(1024)(128)(2,1)S(1)} %dynamic-update-slice), channel_id=1, replica_groups=mesh['bin'=16,'dist'=8] {'bin'}, use_global_device_ids=true, to_apply=%add | all-reduce | flops 1536 | bytes 6144
  78.1 8.0 %all-gather.2.cloned.1.call-done = bf16[1536,512]{1,0:T(8,128)(2,1)} async-done(((bf16[96,512]{1,0:T(8,128)(2,1)}), bf16[1536,512]{1,0:T(8,128)(2,1)}) %all-gather.2.cloned.1.call-update) | async-done | bytes 1572880 | tf_op jit(solution)/shard_map/all_gather | solution.py:58
  86.1 88.6 %while.10 = (s32[]{:T(128)}, bf16[8,8,64,1024]{3,2,1,0:T(8,128)(2,1)}, s32[8,8]{1,0:T(8,128)S(1)}, bf16[48,32,512]{2,1,0:T(8,128)(2,1)}, s32[8,8]{1,0:T(8,128)S(...) while((s32[]{:T(128)}, bf16[8,8,64,1024]{3,2,1,0:T(8,128)(2,1)}, ...), condition=%wide.region_3.4_spmd, body=%wide.region_2.3_spmd.sunk | while | flops 550293568 | bytes 21909952 | solution.py:44
  89.4 2.0 gather_fusion.2
  91.5 2.0 multiply_convert_fusion.2
  93.5 3.6 fusion.17
  98.5 2.0 gather_fusion.3
  100.5 2.0 gather_fusion.2
  102.6 2.0 multiply_convert_fusion.2
  104.6 3.7 fusion.17
  109.6 2.0 gather_fusion.3
  111.6 2.0 gather_fusion.2
  113.7 2.0 multiply_convert_fusion.2
  115.7 3.6 fusion.17
  120.7 2.0 gather_fusion.3
  124.8 2.0 multiply_convert_fusion.2
  126.8 3.6 fusion.17
  133.7 2.0 gather_fusion.2
  135.8 2.0 multiply_convert_fusion.2
  137.8 3.6 fusion.17
  142.8 2.0 gather_fusion.3
  146.9 2.0 multiply_convert_fusion.2
  148.9 3.7 fusion.17
  158.0 2.0 multiply_convert_fusion.2
  160.0 3.6 fusion.17
  169.0 2.0 multiply_convert_fusion.2
  171.0 3.6 fusion.17
  174.7 6.1 %broadcast_in_dim.7 = bf16[128,64,1024]{2,1,0:T(8,128)(2,1)} broadcast(bf16[]{:T(256)} %constant.8.clone.1), dimensions={} | broadcast | bytes 16777218 | tf_op jit(solution)/shard_map/broadcast_in_dim | solution.py:71
  180.8 21.9 %scatter_fusion = bf16[128,64,1024]{2,1,0:T(8,128)(2,1)} fusion(bf16[128,64,1024]{2,1,0:T(8,128)(2,1)} %broadcast_in_dim.7, s32[64]{0:T(128)S(1)} %fusion.8, bf16[64,64,1024]{2,1,0:T(8,128)(2,1)} %bitcast.59), kind=kCustom, calls=%fused_computation.4 | custom fusion | bytes 25166080 | tf_op jit(solution)/shard_map/scatter | solution.py:73
  202.7 189.4 %all_to_all.5 = bf16[128,64,1024]{2,1,0:T(8,128)(2,1)S(1)} all-to-all(bf16[128,64,1024]{2,1,0:T(8,128)(2,1)} %scatter_fusion), channel_id=1, replica_groups=mesh['bin'=16,'dist'=8] {'bin'}, dimensions={0} | all-to-all | bytes 33554432 | tf_op jit(solution)/shard_map/all_to_all | solution.py:75
  392.1 6.2 %copy.28 = bf16[128,64,1024]{2,1,0:T(8,128)(2,1)} copy(bf16[128,64,1024]{2,1,0:T(8,128)(2,1)S(1)} %all_to_all.5) | data formatting | bytes 33554432
  (136 shorter events, 33.9 us)
Async XLA Ops:
  6.5 79.6 %all-gather.2.cloned.1.call-start = ((), (), s32[]{:S(2)}) async-start(), calls=%async_computation.1 | async-start | bytes 1671168 | tf_op jit(solution)/shard_map/all_gather | solution.py:58
  86.1 7.4 %copy-start = (bf16[512,64]{0,1:T(8,128)(2,1)S(1)}, bf16[512,64]{0,1:T(8,128)(2,1)}, u32[]{:S(2)}) copy-start(bf16[512,64]{0,1:T(8,128)(2,1)} %get-tuple-element.128) | copy-start | bytes 196612 | tf_op jit(solution)/shard_map/while
  97.2 7.4 %copy-start = (bf16[512,64]{0,1:T(8,128)(2,1)S(1)}, bf16[512,64]{0,1:T(8,128)(2,1)}, u32[]{:S(2)}) copy-start(bf16[512,64]{0,1:T(8,128)(2,1)} %get-tuple-element.128) | copy-start | bytes 196612 | tf_op jit(solution)/shard_map/while
  108.3 7.4 %copy-start = (bf16[512,64]{0,1:T(8,128)(2,1)S(1)}, bf16[512,64]{0,1:T(8,128)(2,1)}, u32[]{:S(2)}) copy-start(bf16[512,64]{0,1:T(8,128)(2,1)} %get-tuple-element.128) | copy-start | bytes 196612 | tf_op jit(solution)/shard_map/while
  119.3 7.4 %copy-start = (bf16[512,64]{0,1:T(8,128)(2,1)S(1)}, bf16[512,64]{0,1:T(8,128)(2,1)}, u32[]{:S(2)}) copy-start(bf16[512,64]{0,1:T(8,128)(2,1)} %get-tuple-element.128) | copy-start | bytes 196612 | tf_op jit(solution)/shard_map/while
  130.4 7.4 %copy-start = (bf16[512,64]{0,1:T(8,128)(2,1)S(1)}, bf16[512,64]{0,1:T(8,128)(2,1)}, u32[]{:S(2)}) copy-start(bf16[512,64]{0,1:T(8,128)(2,1)} %get-tuple-element.128) | copy-start | bytes 196612 | tf_op jit(solution)/shard_map/while
  141.4 7.4 %copy-start = (bf16[512,64]{0,1:T(8,128)(2,1)S(1)}, bf16[512,64]{0,1:T(8,128)(2,1)}, u32[]{:S(2)}) copy-start(bf16[512,64]{0,1:T(8,128)(2,1)} %get-tuple-element.128) | copy-start | bytes 196612 | tf_op jit(solution)/shard_map/while
  152.5 7.4 %copy-start = (bf16[512,64]{0,1:T(8,128)(2,1)S(1)}, bf16[512,64]{0,1:T(8,128)(2,1)}, u32[]{:S(2)}) copy-start(bf16[512,64]{0,1:T(8,128)(2,1)} %get-tuple-element.128) | copy-start | bytes 196612 | tf_op jit(solution)/shard_map/while
  163.6 7.4 %copy-start = (bf16[512,64]{0,1:T(8,128)(2,1)S(1)}, bf16[512,64]{0,1:T(8,128)(2,1)}, u32[]{:S(2)}) copy-start(bf16[512,64]{0,1:T(8,128)(2,1)} %get-tuple-element.128) | copy-start | bytes 196612 | tf_op jit(solution)/shard_map/while
Sparse Core Ops, SparseCore 0:
  32.2 53.8 all-gather.1
where the time goes:
time: 406 us; the launch traced here: 405 us
  blocking collectives  254 us (63%)
  local copies, waits for them, and re-layouts  77.9 us (19%)
  matrix products  29 us (7%)
  other arithmetic  21.8 us (5%)
  between operations  14 us (3%)
  waiting for transfers between devices  8.05 us (2%)
    all_to_all x1, blocking collectives, per_device(): lax.all_to_all(outbox, 'bin', split_axis=0, concat_axis=0, tiled=True)  189 us
    unnamed x1, blocking collectives  39.3 us
    dot_general x8, matrix products, tile_forms(): jnp.einsum('rd,krq->kdq', kernel, pair_bf, preferred_element_type=jnp.flo...  29 us
    all_gather x1, blocking collectives, per_device(): whole_wave = lax.all_gather(wavefuncs, 'dist', axis=1, tiled=True)  24.8 us
    scatter x1, local copies, waits for them, and re-layouts, per_device(): outbox = jnp.zeros((group_count * capacity, dist_local, TB * TB), jnp.bfl...  21.9 us
    convert_element_type x8, other arithmetic, tile_forms(): (product * angular(row_label, col_label)[:, None]).astype(jnp.bfloat16)  15.9 us
    gather x8, local copies, waits for them, and re-layouts, block_fn(): tile_wave[col_piece]  15.8 us
    gather x8, local copies, waits for them, and re-layouts, block_fn(): tile_wave[row_piece]  15.8 us
  transfers between devices with their start and end apart: 1, of which 1 were waited for; matrix products, arithmetic and copies ran while one was open for 1% of the time, Pallas kernels for 0%

commit v1 on v0

v1 whole, which is shorter than its diff:
```python
import functools
import jax
import jax.numpy as jnp
from jax import lax
from jax.experimental import pallas as pl
from jax.experimental.pallas import tpu as pltpu
from jax.sharding import PartitionSpec as P

D = 64
RPT = 3
CAP = 8
NS = 16
BF = jnp.bfloat16
F32 = jnp.float32
MESH = pl.DeviceIdType.MESH


def gather_kernel(wave, kern, labels, rows, cols, owners, b0, b1, b2, meta, kt,
                  table, z_send, z_recv, m_send, m_recv, c_send, c_recv):
    own, own_d = lax.axis_index("bin"), lax.axis_index("dist")
    x, yh, core = own // 4, (own // 2) % 2, own % 2
    z, yl = own_d // 2, own_d % 2
    y = yh * 2 + yl
    other = 1 - core

    def chip(px, py, pz, pc):
        return (px * 4 + (py // 2) * 2 + pc, pz * 2 + py % 2)

    def up(v, o):
        return (v + o) % 4

    barrier = pltpu.get_barrier_semaphore()
    peers = [((own + k) % NS, own_d) for k in range(1, NS)]
    peers += [chip(x, y, up(z, o), core) for o in (1, 2, 3)]
    peers += [chip(x, up(y, o), z, core) for o in (1, 3)]
    for peer in peers:
        pl.semaphore_signal(barrier, inc=1, device_id=peer, device_id_type=MESH)

    for rt, b in enumerate((b0, b1, b2)):
        part = jnp.concatenate(
            [wave[rt * 32 : rt * 32 + 16, :], wave[rt * 32 + 16 : rt * 32 + 32, :]], axis=1
        )
        if rt == 0:
            b[core, x, y, z] = part
        elif rt == 1:
            b[core, z, x, y] = part
        else:
            b[core, y, z, x] = part

    eye = lax.broadcasted_iota(jnp.int32, (64, 64), 0) == lax.broadcasted_iota(jnp.int32, (64, 64), 1)
    before = lax.broadcasted_iota(jnp.int32, (64, 64), 0) < lax.broadcasted_iota(jnp.int32, (64, 64), 1)

    def column(row):
        return jnp.sum(jnp.where(eye, jnp.broadcast_to(row, (64, 64)), 0), axis=1, keepdims=True)

    own_c = jnp.broadcast_to(owners[...], (64, 64))
    own_r = jnp.sum(jnp.where(eye, own_c, 0), axis=0, keepdims=True)
    rt_r, col_r = rows[...], cols[...]
    rt_c = jnp.broadcast_to(column(rt_r), (64, 64))
    same = (own_c == own_r) & before
    slot_r = jnp.sum(jnp.where(same, 1, 0), axis=0, keepdims=True)
    rank_r = jnp.sum(jnp.where(same & (rt_c == rt_r), 1, 0), axis=0, keepdims=True)
    third = lax.shift_right_logical(col_r * 171, 9)
    tile_r = (col_r - 3 * third) * 16 + third
    key_c = column(rt_r * 8 + rank_r)
    code_c = column(1 + tile_r * 8 + slot_r)
    lane64 = lax.broadcasted_iota(jnp.int32, (64, 128), 1)
    lane1 = lax.broadcasted_iota(jnp.int32, (1, 128), 1)
    spread = jnp.where(lane64 == key_c, jnp.broadcast_to(code_c, (64, 128)), 0)
    label_row = labels[...]
    for o in range(NS):
        mine = jnp.where(owners[...] == o, spread, 0)
        table[o] = jnp.where(lane1 < 32, jnp.sum(mine, axis=0, keepdims=True), label_row)

    meta[own] = table[own]

    pl.semaphore_wait(barrier, len(peers))

    def copy(src, dst, send, recv, device):
        return pltpu.make_async_remote_copy(
            src_ref=src, dst_ref=dst, send_sem=send, recv_sem=recv, device_id=device, device_id_type=MESH
        )

    sent = []

    def block(rt, stage, v, c):
        if rt == 0:
            return (b0.at[c, x, y, v], b0.at[c, x, v], b0.at[c, v])[stage]
        if rt == 1:
            return (b1.at[c, z, x, v], b1.at[c, z, v], b1.at[c, v])[stage]
        return (b2.at[c, y, z, v], b2.at[c, y, v], b2.at[c, v])[stage]

    def place(rt, stage):
        axis = ("zyx", "yxz", "xzy")[rt][stage]
        return {"x": x, "y": y, "z": z}[axis], axis

    def device(axis, v):
        return chip(v if axis == "x" else x, v if axis == "y" else y, v if axis == "z" else z, core)

    def push(rt, stage):
        at, axis = place(rt, stage)
        for o in (1, 3, 2):
            cp = copy(block(rt, stage, at, core), block(rt, stage, at, core),
                      z_send.at[rt, stage, o - 1], z_recv.at[rt, stage, o - 1], device(axis, up(at, o)))
            cp.start()
            sent.append(cp)

    def landed(rt, stage, o):
        at, axis = place(rt, stage)
        v = up(at, 4 - o)
        copy(block(rt, stage, v, core), block(rt, stage, v, core),
             z_send.at[rt, stage, o - 1], z_recv.at[rt, stage, o - 1], device(axis, v)).wait_recv()
        return v

    def across(rt, k, v, c):
        return copy(block(rt, 2, v, c), block(rt, 2, v, c), c_send.at[rt, k], c_recv.at[rt, k], chip(x, y, z, other))

    for rt in range(RPT):
        push(rt, 0)
    for k in range(1, NS):
        to = (own + k) % NS
        cp = copy(table.at[to], meta.at[own], m_send.at[k], m_recv.at[k], (to, own_d))
        cp.start()
        sent.append(cp)
    kt[...] = kern[...].astype(F32).T.astype(BF)
    for rt in range(RPT):
        for o in (1, 3, 2):
            landed(rt, 0, o)
        push(rt, 1)
    for rt in range(RPT):
        for o in (1, 3, 2):
            landed(rt, 1, o)
        push(rt, 2)
        cp = across(rt, 0, place(rt, 2)[0], core)
        cp.start()
        sent.append(cp)
    for o in (1, 3, 2):
        for rt in range(RPT):
            v = landed(rt, 2, o)
            cp = across(rt, o, v, core)
            cp.start()
            sent.append(cp)
    for k in range(1, NS):
        at = (own + NS - k) % NS
        copy(table.at[at], meta.at[at], m_send.at[k], m_recv.at[k], (at, own_d)).wait_recv()
    for o in (0, 1, 3, 2):
        for rt in range(RPT):
            across(rt, o, up(place(rt, 2)[0], (4 - o) % 4), other).wait_recv()
    for cp in sent:
        cp.wait_send()


def swap_blocks(lane, x):
    half=lane<64
    even=(lane//32)%2==0
    def cross(p,q,shift,mask):
        return jnp.where(mask,p,pltpu.roll(q,shift,1)), jnp.where(mask,pltpu.roll(p,128-shift,1),q)
    a0,a2=cross(x[0],x[2],64,half)
    a1,a3=cross(x[1],x[3],64,half)
    y0,y1=cross(a0,a1,32,even)
    y2,y3=cross(a2,a3,32,even)
    return y0,y1,y2,y3

def forms_kernel(msm, mv, kt_ref, b0, b1, b2, out, W, OUT, S1, ANG, LT, sem):
    lane16=lax.broadcasted_iota(jnp.int32,(16,128),1)
    lane=lax.broadcasted_iota(jnp.int32,(64,128),1)
    lo=lane16<64
    for rt,b in enumerate((b0,b1,b2)):
        for x in range(4):
            for yh in range(2):
                for c in range(2):
                    s=x*4+yh*2+c
                    for z in range(4):
                        def at(yl):
                            y=yh*2+yl
                            return b[c,x,y,z] if rt==0 else (b[c,z,x,y] if rt==1 else b[c,y,z,x])
                        p,q=at(0),at(1)
                        W[rt*16+s,0:16,z*128:(z+1)*128]=jnp.concatenate([p[:,:64],q[:,:64]],axis=1)
                        W[rt*16+s,16:32,z*128:(z+1)*128]=jnp.concatenate([p[:,64:],q[:,64:]],axis=1)
    m=mv[...].astype(F32).reshape(16,128)
    rolls=[m]+[pltpu.roll(m,32*k,1) for k in (1,2,3)]
    for rt in range(RPT):
        acc=rolls[(0-rt-1)%4]
        for g in (1,2,3):
            acc=jnp.where(lane16//32==g,rolls[(g-rt-1)%4],acc)
        LT[rt]=acc

    def sender(s, accs, first):
        buf=lax.rem(s,2)
        kt=kt_ref[...]
        dests=[]
        for rt in range(RPT):
            tau=[];dst=[]
            for n in range(CAP):
                code=msm[s,0,rt*8+n]
                ok=code>0
                cm=jnp.maximum(code-1,0)
                tau.append(cm>>3)
                dst.append(jnp.where(ok,cm&7,8))
            dests.append((tau,dst))
        eye=(lax.broadcasted_iota(jnp.int32,(32,128),1)==lax.broadcasted_iota(jnp.int32,(32,128),0))
        for rt in range(RPT):
            tau,_=dests[rt]
            lrow=LT[rt,pl.ds(s,1),:]
            li=jnp.sum(jnp.where(eye,jnp.broadcast_to(lrow,(32,128)),0.0),axis=1,keepdims=True)
            li=jnp.broadcast_to(li,(32,128))
            for h in range(2):
                lj=None
                for g in range(4):
                    t=tau[h*4+g]
                    row=LT[t>>4,pl.ds(t&15,1),:]
                    lj=row if lj is None else jnp.where(lane[0:1]//32==g,row,lj)
                lj=jnp.broadcast_to(lj,(32,128))
                ANG[rt,:,h*128:(h+1)*128]=jnp.sqrt((2.0*li+1.0)*(2.0*lj+1.0))/(8.0*(1.0+jnp.abs(li-lj)))
        def push(rt):
            cols=jnp.concatenate([W[dests[rt][0][n]] for n in range(CAP)],axis=0)
            for mx in range(2):
                pltpu.matmul_push_rhs(cols[:,mx*256:(mx+1)*256],rt%2,mx,transpose=True)
        def issue(q):
            rt,c=divmod(q,8)
            for i4 in range(4):
                i=c*4+i4
                lhs=W[rt*16+s,i:i+1,:]*kt
                for mx in range(2):
                    pltpu.matmul_acc_lhs(accs[mx][q%2][i4],lhs[:,mx*256:(mx+1)*256],load_staged_rhs=(rt%2) if (c==0 and i4==0) else None)
        def post(q):
            rt,c=divmod(q,8)
            xs=[]
            for i4 in range(4):
                i=c*4+i4
                f=(pltpu.matmul_pop(accs[0][q%2][i4])+pltpu.matmul_pop(accs[1][q%2][i4]))*ANG[rt,i:i+1,:]
                f=f.astype(BF)
                xs.append(f[:,:128])
                S1[rt,i]=f[:,128:]
            ys=swap_blocks(lane,xs)
            for n in range(4):
                OUT[buf,dests[rt][1][n],:,c*128:(c+1)*128]=ys[n]
        NQ=RPT*8
        push(0)
        issue(0)
        for q in range(1,NQ):
            if q%8==4 and q//8+1<RPT: push(q//8+1)
            issue(q)
            post(q-1)
        post(NQ-1)
        for rt in range(RPT):
            @pl.when(msm[s,0,rt*8+4]>0)
            def _():
                dd=dests[rt][1]
                def more(c,_):
                    ys=swap_blocks(lane,[S1[rt,c*4+k] for k in range(4)])
                    for n in range(4):
                        OUT[buf,dd[4+n],:,pl.ds(pl.multiple_of(c*128,128),128)]=ys[n]
                    return 0
                lax.fori_loop(0,8,more,0)
        return 0
    def whole(*flat):
        accs=[[flat[0:4],flat[4:8]],[flat[8:12],flat[12:16]]]
        def copy(s,buf):
            return pltpu.make_async_copy(OUT.at[buf,pl.ds(0,8)],out.at[pl.ds(s*8,8)],sem.at[buf])
        def step(s,_):
            buf=lax.rem(s,2)
            @pl.when(s>=2)
            def _(): copy(s-2,buf).wait()
            cnt=jnp.int32(0)
            for rt in range(RPT):
                for n in range(CAP):
                    cnt=cnt+jnp.where(msm[s,0,rt*8+n]>0,1,0)
            for t in range(CAP):
                @pl.when(t>=cnt)
                def _(): OUT[buf,t]=jnp.zeros((D,1024),BF)
            @pl.when(cnt>0)
            def _(): sender(s,accs,None)
            copy(s,buf).start()
            return 0
        lax.fori_loop(0,NS,step,0)
        copy(14,0).wait(); copy(15,1).wait()
    pl.run_scoped(whole,*[pltpu.ACC(mx)((64,256),F32) for mx in range(2) for _ in range(8)])


def gather(wave, kern, labels, rows, cols, owners):
    vm = pl.BlockSpec(memory_space=pltpu.VMEM)
    blocks = jax.ShapeDtypeStruct((2, 4, 4, 4, 16, 128), BF)
    dma = pltpu.SemaphoreType.DMA
    return pl.pallas_call(
        gather_kernel,
        in_specs=[vm] * 6,
        out_specs=[vm] * 5,
        out_shape=[blocks] * 3
        + [jax.ShapeDtypeStruct((NS, 1, 128), jnp.int32), jax.ShapeDtypeStruct((D, 512), BF)],
        scratch_shapes=[
            pltpu.VMEM((NS, 1, 128), jnp.int32),
            dma((3, 3, 3)), dma((3, 3, 3)), dma((NS,)), dma((NS,)), dma((3, 4)), dma((3, 4)),
        ],
        compiler_params=pltpu.CompilerParams(
            collective_id=0, has_side_effects=True, vmem_limit_bytes=24 * 2**20
        ),
    )(wave, kern, labels, rows, cols, owners)


def forms(meta, kt, b0, b1, b2):
    vm = pl.BlockSpec(memory_space=pltpu.VMEM)
    return pl.pallas_call(
        forms_kernel,
        in_specs=[pl.BlockSpec(memory_space=pltpu.SMEM), vm, vm, vm, vm, vm],
        out_specs=pl.BlockSpec(memory_space=pltpu.HBM),
        out_shape=jax.ShapeDtypeStruct((NS * CAP, D, 1024), BF),
        scratch_shapes=[
            pltpu.VMEM((48, 32, 512), BF),
            pltpu.VMEM((2, 9, D, 1024), BF),
            pltpu.VMEM((RPT, 32, D, 128), BF),
            pltpu.VMEM((RPT, 32, 256), F32),
            pltpu.VMEM((RPT, NS, 128), F32),
            pltpu.SemaphoreType.DMA((2,)),
        ],
        compiler_params=pltpu.CompilerParams(vmem_limit_bytes=40 * 2**20),
    )(meta, meta, kt, b0, b1, b2)


def per_device(wavefuncs, kernel, labels, row_tiles, col_tiles, owners):
    label_row = jnp.pad(labels.reshape(1, 96), ((0, 0), (32, 0)))
    b0, b1, b2, meta, kt = gather(
        wavefuncs, kernel, label_row, row_tiles.reshape(1, 64), col_tiles.reshape(1, 64), owners
    )
    return forms(meta, kt, b0, b1, b2)


def solution(mesh):
    return jax.shard_map(
        per_device,
        mesh=mesh,
        in_specs=(P("bin", "dist"), P(None, "dist"), P("bin"), P("bin"), P("bin"), P("bin", None)),
        out_specs=P("bin", "dist", None),
        check_vma=False,
    )
```

time: 406 us -> 71.6 us (0.18)
  the two profiles are of different devices: /device:TPU:1 before, /device:TPU:2 now
where the time goes in v1:
time: 71.6 us; the launch traced here: 71.3 us
  Pallas kernels  66.7 us (93%)
  local copies, waits for them, and re-layouts  4.56 us (6%)
    pallas_call x1, Pallas kernels, forms(): pl.pallas_call(forms_kernel, in_specs=[pl.BlockSpec(memory_space=pltpu.SM...  46.1 us
    pallas_call x1, Pallas kernels, gather(): pl.pallas_call(gather_kernel, in_specs=[vm] * 6, out_specs=[vm] * 5, out_...  20.7 us
    unnamed x7, local copies, waits for them, and re-layouts  3.83 us

profile of v1, /device:TPU:2, one launch (start us, length us, event | category | flops | bytes accessed | tf_op | source)
XLA Modules:
  0.0 71.3 jit_solution(11110050995221415212)
XLA Ops:
  0.0 0.7 %pad.4.labels = s32[1,128]{1,0:T(1,128)S(1)} pad(s32[1,96]{1,0:T(1,128)} %bitcast.5, s32[]{:T(128)} %constant.0.clone.1), padding=0_0x32_0 | pad | bytes 900 | tf_op jit(solution)/shard_map/jit(_pad)/pad | solution.py:321
  0.7 0.8 %copy.7.wave = bf16[96,64]{1,0:T(8,128)(2,1)S(1)} copy(bf16[96,64]{0,1:T(8,128)(2,1)} %param.6) | data formatting | bytes 24576 | tf_op args[0]
  1.5 0.8 %copy.9.owners = s32[64,1]{1,0:T(8,128)S(1)} copy(s32[64,1]{0,1:T(1,128)} %param.11) | data formatting | bytes 512 | tf_op args[5]
  2.3 1.0 %copy.8.kern = bf16[512,64]{1,0:T(8,128)(2,1)S(1)} copy(bf16[512,64]{0,1:T(8,128)(2,1)} %param.7) | data formatting | bytes 131072 | tf_op args[1]
  3.3 0.0 copy-start
  3.3 0.6 copy-done
  3.9 0.0 copy-start.1
  3.9 0.7 copy-done.1
  4.6 20.7 %shard_map.64 = (bf16[2,4,4,4,16,128]{5,4,3,2,1,0:T(8,128)(2,1)S(1)}, bf16[2,4,4,4,16,128]{5,4,3,2,1,0:T(8,128)(2,1)S(1)}, bf16[2,4,4,4,16,128]{5,4,3,2,1,0:T(8,...) custom-call(bf16[96,64]{1,0:T(8,128)(2,1)S(1)} %copy.7.wave, bf16[512,64]{1,0:T(8,128)(2,1)S(1)} %copy.8.kern, ...), custom_call_target="tpu_custom_call" | custom-call | tf_op jit(solution)/shard_map/pallas_call | solution.py:285
  25.3 46.1 %shard_map.65 = bf16[128,64,1024]{2,1,0:T(8,128)(2,1)} custom-call(s32[16,1,128]{2,1,0:T(1,128)S(1)} %get-tuple-element.10.msm.mv, s32[16,1,128]{2,1,0:T(1,128)S(1)} %get-tuple-element.10.msm.mv, bf16[64,512]{1,0:T(8,128)(2,1)S(1)} %get-tuple-element.11.kt_ref, bf16[2,4,4,4,16,128]{5,4,3,2,1,0:T(8,128)(2,1)S(1)} %get-tuple-element.12.b0, ...), custom_call_target="tpu_custom_call" | custom-call | tf_op jit(solution)/shard_map/pallas_call | solution.py:303
Async XLA Ops:
  3.3 0.7 copy-start
  3.9 0.7 copy-start.1

commit v2 on v1

v2 whole, which is shorter than its diff:
```python
import functools
import jax
import jax.numpy as jnp
from jax import lax
from jax.experimental import pallas as pl
from jax.experimental.pallas import tpu as pltpu
from jax.sharding import PartitionSpec as P

D = 64
RPT = 3
CAP = 8
NS = 16
BF = jnp.bfloat16
F32 = jnp.float32
MESH = pl.DeviceIdType.MESH


def gather_kernel(wave_in, labels_in, rows_in, cols_in, owners_in, b0, b1, b2, meta,
                  table, wave, labels, rows, cols, owners, in_sem,
                  z_send, z_recv, m_send, m_recv, c_send, c_recv):
    loads = [
        pltpu.make_async_copy(src, dst, in_sem.at[k])
        for k, (src, dst) in enumerate(
            ((wave_in, wave), (labels_in, labels), (rows_in, rows), (cols_in, cols), (owners_in, owners))
        )
    ]
    for load in loads:
        load.start()
    own, own_d = lax.axis_index("bin"), lax.axis_index("dist")
    x, yh, core = own // 4, (own // 2) % 2, own % 2
    z, yl = own_d // 2, own_d % 2
    y = yh * 2 + yl
    other = 1 - core

    def chip(px, py, pz, pc):
        return (px * 4 + (py // 2) * 2 + pc, pz * 2 + py % 2)

    def up(v, o):
        return (v + o) % 4

    barrier = pltpu.get_barrier_semaphore()
    peers = [((own + k) % NS, own_d) for k in range(1, NS)]
    peers += [chip(x, y, up(z, o), core) for o in (1, 2, 3)]
    peers += [chip(x, up(y, o), z, core) for o in (1, 3)]
    for peer in peers:
        pl.semaphore_signal(barrier, inc=1, device_id=peer, device_id_type=MESH)

    for load in loads:
        load.wait()
    shard = wave[...].astype(F32).T
    for rt, b in enumerate((b0, b1, b2)):
        part = jnp.concatenate(
            [shard[rt * 32 : rt * 32 + 16, :], shard[rt * 32 + 16 : rt * 32 + 32, :]], axis=1
        ).astype(BF)
        if rt == 0:
            b[core, x, y, z] = part
        elif rt == 1:
            b[core, z, x, y] = part
        else:
            b[core, y, z, x] = part

    sub64 = lax.broadcasted_iota(jnp.int32, (64, 64), 0)
    lan64 = lax.broadcasted_iota(jnp.int32, (64, 64), 1)

    def column(row):
        return jnp.sum(jnp.where(sub64 == lan64, jnp.broadcast_to(row, (64, 64)), 0), axis=1, keepdims=True)

    own_r, col_r = owners[...], cols[...]
    own_c = column(own_r)
    same = (jnp.broadcast_to(own_c, (64, 64)) == own_r) & (lan64 < sub64)
    slot_c = jnp.sum(jnp.where(same, 1, 0), axis=1, keepdims=True)
    third = lax.shift_right_logical(col_r * 171, 9)
    code_c = column(1 + rows[...] * 64 + (col_r - 3 * third) * 16 + third)
    lane64 = lax.broadcasted_iota(jnp.int32, (64, 128), 1)
    lane1 = lax.broadcasted_iota(jnp.int32, (1, 128), 1)
    spread = jnp.where(lane64 == slot_c, jnp.broadcast_to(code_c, (64, 128)), 0)
    label_row = jnp.concatenate([jnp.zeros((1, 32), jnp.int32), labels[...]], axis=1)
    for o in range(NS):
        mine = jnp.where(own_c == o, spread, 0)
        table[o] = jnp.where(lane1 < 32, jnp.sum(mine, axis=0, keepdims=True), label_row)

    meta[own] = table[own]

    pl.semaphore_wait(barrier, len(peers))

    def copy(src, dst, send, recv, device):
        return pltpu.make_async_remote_copy(
            src_ref=src, dst_ref=dst, send_sem=send, recv_sem=recv, device_id=device, device_id_type=MESH
        )

    sent = []

    def block(rt, stage, v, c):
        if rt == 0:
            return (b0.at[c, x, y, v], b0.at[c, x, v], b0.at[c, v])[stage]
        if rt == 1:
            return (b1.at[c, z, x, v], b1.at[c, z, v], b1.at[c, v])[stage]
        return (b2.at[c, y, z, v], b2.at[c, y, v], b2.at[c, v])[stage]

    def place(rt, stage):
        axis = ("zyx", "yxz", "xzy")[rt][stage]
        return {"x": x, "y": y, "z": z}[axis], axis

    def device(axis, v):
        return chip(v if axis == "x" else x, v if axis == "y" else y, v if axis == "z" else z, core)

    def push(rt, stage):
        at, axis = place(rt, stage)
        for o in (1, 3, 2):
            cp = copy(block(rt, stage, at, core), block(rt, stage, at, core),
                      z_send.at[rt, stage, o - 1], z_recv.at[rt, stage, o - 1], device(axis, up(at, o)))
            cp.start()
            sent.append(cp)

    def landed(rt, stage, o):
        at, axis = place(rt, stage)
        v = up(at, 4 - o)
        copy(block(rt, stage, v, core), block(rt, stage, v, core),
             z_send.at[rt, stage, o - 1], z_recv.at[rt, stage, o - 1], device(axis, v)).wait_recv()
        return v

    def across(rt, k, v, c):
        return copy(block(rt, 2, v, c), block(rt, 2, v, c), c_send.at[rt, k], c_recv.at[rt, k], chip(x, y, z, other))

    for rt in range(RPT):
        push(rt, 0)
    for k in range(1, NS):
        to = (own + k) % NS
        cp = copy(table.at[to], meta.at[own], m_send.at[k], m_recv.at[k], (to, own_d))
        cp.start()
        sent.append(cp)
    for rt in range(RPT):
        for o in (1, 3, 2):
            landed(rt, 0, o)
        push(rt, 1)
    for rt in range(RPT):
        for o in (1, 3, 2):
            landed(rt, 1, o)
        push(rt, 2)
        cp = across(rt, 0, place(rt, 2)[0], core)
        cp.start()
        sent.append(cp)
    for o in (1, 3, 2):
        for rt in range(RPT):
            v = landed(rt, 2, o)
            cp = across(rt, o, v, core)
            cp.start()
            sent.append(cp)
    for k in range(1, NS):
        at = (own + NS - k) % NS
        copy(table.at[at], meta.at[at], m_send.at[k], m_recv.at[k], (at, own_d)).wait_recv()
    for o in (0, 1, 3, 2):
        for rt in range(RPT):
            across(rt, o, up(place(rt, 2)[0], (4 - o) % 4), other).wait_recv()
    for cp in sent:
        cp.wait_send()


def swap_blocks(lane, x):
    half=lane<64
    even=(lane//32)%2==0
    def cross(p,q,shift,mask):
        return jnp.where(mask,p,pltpu.roll(q,shift,1)), jnp.where(mask,pltpu.roll(p,128-shift,1),q)
    a0,a2=cross(x[0],x[2],64,half)
    a1,a3=cross(x[1],x[3],64,half)
    y0,y1=cross(a0,a1,32,even)
    y2,y3=cross(a2,a3,32,even)
    return y0,y1,y2,y3

def forms_kernel(msm, mv, kt_in, b0, b1, b2, out, W, OUT, ANG, LT, LC, kt_ref, sem):
    load=pltpu.make_async_copy(kt_in,kt_ref,sem.at[2])
    load.start()
    lane16=lax.broadcasted_iota(jnp.int32,(16,128),1)
    lane=lax.broadcasted_iota(jnp.int32,(64,128),1)
    lo=lane16<64
    for rt,b in enumerate((b0,b1,b2)):
        for x in range(4):
            for yh in range(2):
                for c in range(2):
                    s=x*4+yh*2+c
                    for z in range(4):
                        def at(yl):
                            y=yh*2+yl
                            return b[c,x,y,z] if rt==0 else (b[c,z,x,y] if rt==1 else b[c,y,z,x])
                        p,q=at(0),at(1)
                        W[rt*16+s,0:16,z*128:(z+1)*128]=jnp.concatenate([p[:,:64],q[:,:64]],axis=1)
                        W[rt*16+s,16:32,z*128:(z+1)*128]=jnp.concatenate([p[:,64:],q[:,64:]],axis=1)
    m=mv[...].astype(F32).reshape(16,128)
    rolls=[m]+[pltpu.roll(m,32*k,1) for k in (1,2,3)]
    for rt in range(RPT):
        acc=rolls[(0-rt-1)%4]
        for g in (1,2,3):
            acc=jnp.where(lane16//32==g,rolls[(g-rt-1)%4],acc)
        LT[rt]=acc

    W[48]=jnp.zeros((32,512),BF)
    eye=(lax.broadcasted_iota(jnp.int32,(32,128),1)==lax.broadcasted_iota(jnp.int32,(32,128),0))
    blk=lax.broadcasted_iota(jnp.int32,(32,128),1)//32
    load.wait()
    kt=kt_ref[...]
    I8=8

    def codes(s):
        out=[]
        for n in range(CAP):
            code=msm[s,0,n]
            cm=jnp.maximum(code-1,0)
            out.append((code>0,cm>>6,cm&63))
        return out

    def prep(s):
        cs=codes(s)
        for rt in range(RPT):
            lrow=LT[rt,pl.ds(s,1),:]
            li=jnp.sum(jnp.where(eye,jnp.broadcast_to(lrow,(32,128)),0.0),axis=1,keepdims=True)
            LC[rt]=jnp.broadcast_to(li,(32,128))
        for h in range(2):
            lj=li=None
            for g in range(4):
                _,rt,t=cs[h*4+g]
                row=jnp.broadcast_to(LT[t>>4,pl.ds(t&15,1),:],(32,128))
                col=LC[rt]
                lj=row if lj is None else jnp.where(blk==g,row,lj)
                li=col if li is None else jnp.where(blk==g,col,li)
            ANG[lax.rem(s,2),:,h*128:(h+1)*128]=jnp.sqrt((2.0*li+1.0)*(2.0*lj+1.0))/(8.0*(1.0+jnp.abs(li-lj)))

    def push(s,k):
        rt=k%3
        tiles=[W[jnp.where(ok&(r==rt),t,48)] for ok,r,t in codes(s)]
        cols=jnp.concatenate(tiles,axis=0)
        for mx in range(2):
            pltpu.matmul_push_rhs(cols[:,mx*256:(mx+1)*256],k%2,mx,transpose=True)

    def issue(accs,s,k,snext,knext):
        c,rt=divmod(k,3)
        for i8 in range(I8):
            i=c*I8+i8
            lhs=W[rt*16+s,i:i+1,:]*kt
            for mx in range(2):
                pltpu.matmul_acc_lhs(accs[mx][c%2][i8],lhs[:,mx*256:(mx+1)*256],load_staged_rhs=(k%2) if i8==0 else None)
            if i8==0: push(snext,knext)

    def post(accs,s,c,half):
        buf=lax.rem(s,2)
        lows,highs=[],[]
        for i4 in range(4):
            i8=half*4+i4
            i=c*I8+i8
            f=(pltpu.matmul_pop(accs[0][c%2][i8])+pltpu.matmul_pop(accs[1][c%2][i8]))*ANG[buf,i:i+1,:]
            f=f.astype(BF)
            lows.append(f[:,:128]); highs.append(f[:,128:])
        q=c*2+half
        for base,xs in ((0,lows),(4,highs)):
            for n,v in enumerate(swap_blocks(lane,xs)):
                OUT[buf,base+n,:,q*128:(q+1)*128]=v

    def whole(*flat):
        accs=[[flat[mx*16+b*8:mx*16+b*8+8] for b in range(2)] for mx in range(2)]
        def copy(s,buf):
            return pltpu.make_async_copy(OUT.at[buf],out.at[pl.ds(s*8,8)],sem.at[buf])
        prep(0)
        push(0,0)
        issue(accs,0,0,0,1)
        def step(s,_):
            buf=lax.rem(s,2)
            nxt=jnp.minimum(s+1,NS-1)
            @pl.when(s>=2)
            def _(): copy(s-2,buf).wait()
            for k in range(1,13):
                if k<12:
                    issue(accs,s,k,s if k<11 else nxt,(k+1)%12)
                else:
                    issue(accs,nxt,0,nxt,1)
                c,rt=divmod(k,3)
                if c>0 and rt<2 and k<12: post(accs,s,c-1,rt)
                if k==6: prep(nxt)
            post(accs,s,3,0)
            post(accs,s,3,1)
            copy(s,buf).start()
            return 0
        lax.fori_loop(0,NS,step,0)
        for mx in range(2):
            pltpu.matmul_acc_lhs(accs[mx][0][0],kt[:,mx*256:(mx+1)*256],load_staged_rhs=1)
        tot=jnp.zeros((64,256),F32)
        for mx in range(2):
            for i8 in range(I8):
                tot=tot+pltpu.matmul_pop(accs[mx][0][i8])
        ANG[0]=tot[0:32]
        copy(14,0).wait(); copy(15,1).wait()
    pl.run_scoped(whole,*[pltpu.ACC(mx)((64,256),F32) for mx in range(2) for _ in range(16)])


def gather(wave, labels, rows, cols, owners):
    vm = pl.BlockSpec(memory_space=pltpu.VMEM)
    blocks = jax.ShapeDtypeStruct((2, 4, 4, 4, 16, 128), BF)
    dma = pltpu.SemaphoreType.DMA
    return pl.pallas_call(
        gather_kernel,
        in_specs=[pl.BlockSpec(memory_space=pltpu.HBM)] * 5,
        out_specs=[vm] * 4,
        out_shape=[blocks] * 3 + [jax.ShapeDtypeStruct((NS, 1, 128), jnp.int32)],
        scratch_shapes=[
            pltpu.VMEM((NS, 1, 128), jnp.int32),
            pltpu.VMEM((64, 96), BF),
            pltpu.VMEM((1, 96), jnp.int32),
            pltpu.VMEM((1, 64), jnp.int32),
            pltpu.VMEM((1, 64), jnp.int32),
            pltpu.VMEM((1, 64), jnp.int32),
            dma((5,)),
            dma((3, 3, 3)), dma((3, 3, 3)), dma((NS,)), dma((NS,)), dma((3, 4)), dma((3, 4)),
        ],
        compiler_params=pltpu.CompilerParams(
            collective_id=0, has_side_effects=True, vmem_limit_bytes=24 * 2**20
        ),
    )(wave, labels, rows, cols, owners)


def forms(meta, kt, b0, b1, b2):
    vm = pl.BlockSpec(memory_space=pltpu.VMEM)
    return pl.pallas_call(
        forms_kernel,
        in_specs=[pl.BlockSpec(memory_space=pltpu.SMEM), vm, pl.BlockSpec(memory_space=pltpu.HBM), vm, vm, vm],
        out_specs=pl.BlockSpec(memory_space=pltpu.HBM),
        out_shape=jax.ShapeDtypeStruct((NS * CAP, D, 1024), BF),
        scratch_shapes=[
            pltpu.VMEM((49, 32, 512), BF),
            pltpu.VMEM((2, CAP, D, 1024), BF),
            pltpu.VMEM((2, 32, 256), F32),
            pltpu.VMEM((RPT, NS, 128), F32),
            pltpu.VMEM((RPT, 32, 128), F32),
            pltpu.VMEM((D, 512), BF),
            pltpu.SemaphoreType.DMA((3,)),
        ],
        compiler_params=pltpu.CompilerParams(vmem_limit_bytes=40 * 2**20),
    )(meta, meta, kt, b0, b1, b2)


def per_device(wavefuncs, kernel, labels, row_tiles, col_tiles, owners):
    def in_hbm(v):
        return pltpu.with_memory_space_constraint(v, pltpu.HBM)

    b0, b1, b2, meta = gather(
        in_hbm(wavefuncs.T),
        in_hbm(labels.reshape(1, 96)),
        in_hbm(row_tiles.reshape(1, 64)),
        in_hbm(col_tiles.reshape(1, 64)),
        in_hbm(owners.T),
    )
    return forms(meta, in_hbm(kernel.T), b0, b1, b2)


def solution(mesh):
    return jax.shard_map(
        per_device,
        mesh=mesh,
        in_specs=(P("bin", "dist"), P(None, "dist"), P("bin"), P("bin"), P("bin"), P("bin", None)),
        out_specs=P("bin", "dist", None),
        check_vma=False,
    )
```

time: 71.6 us -> 55.4 us (0.77)
  the two profiles are of different devices: /device:TPU:2 before, /device:TPU:1 now
where the time goes in v2:
time: 55.4 us; the launch traced here: 55.2 us
  Pallas kernels  55.2 us (100%)
    pallas_call x1, Pallas kernels, forms(): pl.pallas_call(forms_kernel, in_specs=[pl.BlockSpec(memory_space=pltpu.SM...  32.1 us
    pallas_call x1, Pallas kernels, gather(): pl.pallas_call(gather_kernel, in_specs=[pl.BlockSpec(memory_space=pltpu.H...  23.1 us

profile of v2, /device:TPU:1, one launch (start us, length us, event | category | flops | bytes accessed | tf_op | source)
XLA Modules:
  0.0 55.2 jit_solution(890184736285952876)
XLA Ops:
  0.0 23.1 %shard_map.64 = (bf16[2,4,4,4,16,128]{5,4,3,2,1,0:T(8,128)(2,1)S(1)}, bf16[2,4,4,4,16,128]{5,4,3,2,1,0:T(8,128)(2,1)S(1)}, bf16[2,4,4,4,16,128]{5,4,3,2,1,0:T(8,128)(2,1)S(1)}, s32[16,1,128]{2,1,0:T(1,128)S(1)}) custom-call(bf16[64,96]{1,0:T(8,128)(2,1)} %bitcast.7, s32[1,96]{1,0:T(1,128)} %bitcast.8, s32[1,64]{1,0:T(1,128)} %bitcast.9, s32[1,64]{1,0:T(1,128)} %bitcast.10, ...), custom_call_target="tpu_custom_call" | custom-call | tf_op jit(solution)/shard_map/pallas_call | solution.py:297
  23.1 32.1 %shard_map.65 = bf16[128,64,1024]{2,1,0:T(8,128)(2,1)} custom-call(s32[16,1,128]{2,1,0:T(1,128)S(1)} %get-tuple-element.9.msm.mv, s32[16,1,128]{2,1,0:T(1,128)S(1)} %get-tuple-element.9.msm.mv, bf16[64,512]{1,0:T(8,128)(2,1)} %bitcast.6, bf16[2,4,4,4,16,128]{5,4,3,2,1,0:T(8,128)(2,1)S(1)} %get-tuple-element.10.b0, ...), custom_call_target="tpu_custom_call" | custom-call | tf_op jit(solution)/shard_map/pallas_call | solution.py:320

commit v3 on v2

v3 whole, which is shorter than its diff:
```python
import functools
import jax
import jax.numpy as jnp
from jax import lax
from jax.experimental import pallas as pl
from jax.experimental.pallas import tpu as pltpu
from jax.sharding import PartitionSpec as P

D = 64
RPT = 3
CAP = 8
NS = 16
BF = jnp.bfloat16
F32 = jnp.float32
MESH = pl.DeviceIdType.MESH


def gather_kernel(wave_in, labels_in, rows_in, cols_in, owners_in, kt_in, w_all, lt, meta, kt,
                  b0, b1, b2, table, via_x, via_y, wave, labels, rows, cols, owners, in_sem,
                  z_send, z_recv, c_send, c_recv, m_send, m_recv):
    loads = [
        pltpu.make_async_copy(src, dst, in_sem.at[k])
        for k, (src, dst) in enumerate(
            ((wave_in, wave), (labels_in, labels), (rows_in, rows), (cols_in, cols), (owners_in, owners), (kt_in, kt))
        )
    ]
    for load in loads:
        load.start()
    own, own_d = lax.axis_index("bin"), lax.axis_index("dist")
    x, yh, core = own // 4, (own // 2) % 2, own % 2
    z, yl = own_d // 2, own_d % 2
    y = yh * 2 + yl
    other = 1 - core

    def chip(px, py, pz, pc):
        return (px * 4 + (py // 2) * 2 + pc, pz * 2 + py % 2)

    def up(v, o):
        return (v + o) % 4

    def peer(axis, o):
        return chip(
            up(x, o) if axis == "x" else x, up(y, o) if axis == "y" else y, up(z, o) if axis == "z" else z, core
        )

    barrier = pltpu.get_barrier_semaphore()
    peers = [peer(axis, o) for o in (2, 1, 3) for axis in "xyz"] + [chip(x, y, z, other)]
    for at in peers:
        pl.semaphore_signal(barrier, inc=1, device_id=at, device_id_type=MESH)

    loads[0].wait()
    shard = wave[...].astype(F32).T
    for rt, b in enumerate((b0, b1, b2)):
        part = jnp.concatenate(
            [shard[rt * 32 : rt * 32 + 16, :], shard[rt * 32 + 16 : rt * 32 + 32, :]], axis=1
        ).astype(BF)
        if rt == 0:
            b[core, x, y, z] = part
        elif rt == 1:
            b[core, z, x, y] = part
        else:
            b[core, y, z, x] = part

    pl.semaphore_wait(barrier, len(peers))

    def copy(src, dst, send, recv, device):
        return pltpu.make_async_remote_copy(
            src_ref=src, dst_ref=dst, send_sem=send, recv_sem=recv, device_id=device, device_id_type=MESH
        )

    def taken(ref, send):
        copy(ref, ref, send, send, peers[0]).wait_send()

    def arrived(ref, recv):
        copy(ref, ref, recv, recv, peers[0]).wait_recv()

    def block(rt, stage, v, c):
        if rt == 0:
            return (b0.at[c, x, y, v], b0.at[c, x, v], b0.at[c, v])[stage]
        if rt == 1:
            return (b1.at[c, z, x, v], b1.at[c, z, v], b1.at[c, v])[stage]
        return (b2.at[c, y, z, v], b2.at[c, y, v], b2.at[c, v])[stage]

    def place(rt, stage):
        axis = ("zyx", "yxz", "xzy")[rt][stage]
        return {"x": x, "y": y, "z": z}[axis], axis

    def push(rt, stage):
        at, axis = place(rt, stage)
        mine = block(rt, stage, at, core)
        for o in (2, 1, 3):
            recv = z_recv.at[rt, stage + (stage == 2 and o == 2)]
            copy(mine, mine, z_send.at[rt, stage], recv, peer(axis, o)).start()

    def some(rt, stage, n):
        b = (b0, b1, b2)[rt]
        return (b.at[0, 0, 0, pl.ds(0, n)], b.at[0, 0, pl.ds(0, n)], b.at[0, pl.ds(0, n)])[stage]

    def across(rt, o, k):
        v = up(place(rt, 2)[0], (4 - o) % 4)
        copy(block(rt, 2, v, core), block(rt, 2, v, core), c_send.at[rt], c_recv.at[rt, k], chip(x, y, z, other)).start()

    def lay_stage(rt, c, o):
        if rt < 2:
            lay_plane(rt, up(place(rt, 2)[0], (4 - o) % 4), c)

    def lay(rt, c, px, h, pz, even, odd):
        tile = rt * 16 + c * 8 + h * 4 + px
        lanes = pl.ds(pl.multiple_of(pz * 128, 128), 128)
        w_all[tile, 0:16, lanes] = jnp.concatenate([even[:, :64], odd[:, :64]], axis=1)
        w_all[tile, 16:32, lanes] = jnp.concatenate([even[:, 64:], odd[:, 64:]], axis=1)

    def lay_plane(rt, v, c):
        if rt == 0:
            for h in range(2):
                for pz in range(4):
                    lay(0, c, v, h, pz, b0[c, v, 2 * h, pz], b0[c, v, 2 * h + 1, pz])
        elif rt == 1:
            for px in range(4):
                for h in range(2):
                    lay(1, c, px, h, v, b1[c, v, px, 2 * h], b1[c, v, px, 2 * h + 1])
        else:
            for pz in range(4):
                for px in range(4):
                    lay(2, c, px, v, pz, b2[c, 2 * v, pz, px], b2[c, 2 * v + 1, pz, px])

    for rt in range(RPT):
        push(rt, 0)

    for load in loads[1:]:
        load.wait()
    sub64 = lax.broadcasted_iota(jnp.int32, (64, 64), 0)
    lan64 = lax.broadcasted_iota(jnp.int32, (64, 64), 1)

    def column(row):
        return jnp.sum(jnp.where(sub64 == lan64, jnp.broadcast_to(row, (64, 64)), 0), axis=1, keepdims=True)

    own_r, col_r = owners[...], cols[...]
    own_c = column(own_r)
    same = (jnp.broadcast_to(own_c, (64, 64)) == own_r) & (lan64 < sub64)
    slot_c = jnp.sum(jnp.where(same, 1, 0), axis=1, keepdims=True)
    third = lax.shift_right_logical(col_r * 171, 9)
    number = (third & 1) * 8 + (third & 2) * 2 + lax.shift_right_logical(third, 2)
    code_c = column(1 + rows[...] * 64 + (col_r - 3 * third) * 16 + number)
    lane64 = lax.broadcasted_iota(jnp.int32, (64, 128), 1)
    lane1 = lax.broadcasted_iota(jnp.int32, (1, 128), 1)
    spread = jnp.where(lane64 == slot_c, jnp.broadcast_to(code_c, (64, 128)), 0)
    label_row = jnp.concatenate([jnp.zeros((1, 32), jnp.int32), labels[...]], axis=1)
    for o in range(NS):
        mine = jnp.where(own_c == o, spread, 0)
        table[o // 4, o % 4] = jnp.where(lane1 < 32, jnp.sum(mine, axis=0, keepdims=True), label_row)

    for o in (2, 1, 3):
        copy(table.at[up(x, o)], via_x.at[x], m_send.at[0], m_recv.at[0], peer("x", o)).start()
    via_x[x] = table[x]

    for rt in range(RPT):
        arrived(some(rt, 0, 3), z_recv.at[rt, 0])
        push(rt, 1)
    for rt in range(RPT):
        taken(some(rt, 0, 3), z_send.at[rt, 0])

    arrived(via_x.at[pl.ds(0, 3)], m_recv.at[0])
    taken(table.at[pl.ds(0, 3)], m_send.at[0])
    far = 1 - yh
    meta_y = copy(via_x.at[:, pl.ds(far * 2, 2)], via_y.at[yh], m_send.at[1], m_recv.at[1], peer("y", 2))
    meta_y.start()
    via_y[yh] = via_x[:, pl.ds(yh * 2, 2)]

    for rt in range(RPT):
        arrived(some(rt, 1, 3), z_recv.at[rt, 1])
        push(rt, 2)
        across(rt, 0, 0)
    for rt in range(RPT):
        taken(some(rt, 1, 3), z_send.at[rt, 1])

    arrived(via_y.at[far], m_recv.at[1])
    meta_c = copy(via_y.at[:, :, other], meta.at[core], m_send.at[2], m_recv.at[2], chip(x, y, z, other))
    meta_c.start()
    meta_y.wait_send()
    meta[core] = via_y[:, :, core]
    w_all[48] = jnp.zeros((32, 512), BF)
    lay_plane(0, x, core)
    lay_plane(1, z, core)

    arrived(meta.at[other], m_recv.at[2])
    meta_c.wait_send()
    lane16 = lax.broadcasted_iota(jnp.int32, (NS, 128), 1)
    found = jnp.concatenate([meta[c, h, p] for c in range(2) for h in range(2) for p in range(4)], axis=0)
    found = found.astype(F32)
    rolled = [found] + [pltpu.roll(found, 32 * k, 1) for k in (1, 2, 3)]
    for rt in range(RPT):
        labs = rolled[(0 - rt - 1) % 4]
        for g in (1, 2, 3):
            labs = jnp.where(lane16 // 32 == g, rolled[(g - rt - 1) % 4], labs)
        lt[rt] = labs
    for rt in range(RPT):
        arrived(some(rt, 2, 2), z_recv.at[rt, 2])
        across(rt, 1, 1)
        across(rt, 3, 1)
    for rt in range(RPT):
        arrived(some(rt, 2, 1), c_recv.at[rt, 0])
        lay_stage(rt, other, 0)
        lay_stage(rt, core, 1)
        lay_stage(rt, core, 3)
    lay_plane(2, yh, core)
    for rt in range(RPT):
        arrived(some(rt, 2, 1), z_recv.at[rt, 3])
        across(rt, 2, 2)
    for rt in range(RPT):
        arrived(some(rt, 2, 2), c_recv.at[rt, 1])
        lay_stage(rt, other, 1)
        lay_stage(rt, other, 3)
        lay_stage(rt, core, 2)
    lay_plane(2, yh, other)
    lay_plane(2, far, core)
    for rt in range(RPT):
        taken(some(rt, 2, 3), z_send.at[rt, 2])
    for rt in range(RPT):
        arrived(some(rt, 2, 1), c_recv.at[rt, 2])
        lay_stage(rt, other, 2)
    lay_plane(2, far, other)
    for rt in range(RPT):
        taken(some(rt, 2, 4), c_send.at[rt])


def swap_blocks(lane, x):
    half=lane<64
    even=(lane//32)%2==0
    def cross(p,q,shift,mask):
        return jnp.where(mask,p,pltpu.roll(q,shift,1)), jnp.where(mask,pltpu.roll(p,128-shift,1),q)
    a0,a2=cross(x[0],x[2],64,half)
    a1,a3=cross(x[1],x[3],64,half)
    y0,y1=cross(a0,a1,32,even)
    y2,y3=cross(a2,a3,32,even)
    return y0,y1,y2,y3

def forms_kernel(msm, W, LT, kt_ref, out, OUT, ANG, LC, sem):
    lane=lax.broadcasted_iota(jnp.int32,(64,128),1)
    eye=(lax.broadcasted_iota(jnp.int32,(32,128),1)==lax.broadcasted_iota(jnp.int32,(32,128),0))
    blk=lax.broadcasted_iota(jnp.int32,(32,128),1)//32
    kt=kt_ref[...]
    I8=8

    def codes(s):
        out=[]
        for n in range(CAP):
            code=msm[s,0,n]
            cm=jnp.maximum(code-1,0)
            out.append((code>0,cm>>6,cm&63))
        return out

    def prep(s):
        cs=codes(s)
        for rt in range(RPT):
            lrow=LT[rt,pl.ds(s,1),:]
            li=jnp.sum(jnp.where(eye,jnp.broadcast_to(lrow,(32,128)),0.0),axis=1,keepdims=True)
            LC[rt]=jnp.broadcast_to(li,(32,128))
        for h in range(2):
            lj=li=None
            for g in range(4):
                _,rt,t=cs[h*4+g]
                row=jnp.broadcast_to(LT[t>>4,pl.ds(t&15,1),:],(32,128))
                col=LC[rt]
                lj=row if lj is None else jnp.where(blk==g,row,lj)
                li=col if li is None else jnp.where(blk==g,col,li)
            ANG[lax.rem(s,2),:,h*128:(h+1)*128]=jnp.sqrt((2.0*li+1.0)*(2.0*lj+1.0))/(8.0*(1.0+jnp.abs(li-lj)))

    def rt_of(k):
        c,p=divmod(k%12,3)
        return p if c%2==0 else 2-p
    fresh=[k for k in range(12) if k==0 or rt_of(k)!=rt_of(k-1)]
    def push(s,k):
        rt=rt_of(k)
        tiles=[W[jnp.where(ok&(r==rt),t,48)] for ok,r,t in codes(s)]
        cols=jnp.concatenate(tiles,axis=0)
        for mx in range(2):
            pltpu.matmul_push_rhs(cols[:,mx*256:(mx+1)*256],fresh.index(k)%2,mx,transpose=True)

    def issue(accs,s,k,snext):
        c=k//3
        rt=rt_of(k)
        for i8 in range(I8):
            i=c*I8+i8
            lhs=W[rt*16+s,i:i+1,:]*kt
            for mx in range(2):
                pltpu.matmul_acc_lhs(accs[mx][c%2][i8],lhs[:,mx*256:(mx+1)*256],load_staged_rhs=(fresh.index(k)%2) if i8==0 and k in fresh else None)
            if i8==0 and k in fresh:
                j=fresh.index(k)+1
                push(s if j<len(fresh) else snext,fresh[j%len(fresh)])

    def post(accs,s,c,half):
        buf=lax.rem(s,2)
        lows,highs=[],[]
        for i4 in range(4):
            i8=half*4+i4
            i=c*I8+i8
            f=(pltpu.matmul_pop(accs[0][c%2][i8])+pltpu.matmul_pop(accs[1][c%2][i8]))*ANG[buf,i:i+1,:]
            f=f.astype(BF)
            lows.append(f[:,:128]); highs.append(f[:,128:])
        q=c*2+half
        for base,xs in ((0,lows),(4,highs)):
            for n,v in enumerate(swap_blocks(lane,xs)):
                OUT[buf,base+n,:,q*128:(q+1)*128]=v

    def whole(*flat):
        accs=[[flat[mx*16+b*8:mx*16+b*8+8] for b in range(2)] for mx in range(2)]
        def copy(s,buf):
            place=(s%4)*4+((s//4)%2)*2+s//8
            return pltpu.make_async_copy(OUT.at[buf],out.at[pl.ds(place*8,8)],sem.at[buf])
        prep(0)
        push(0,0)
        issue(accs,0,0,0)
        def step(s,_):
            buf=lax.rem(s,2)
            nxt=jnp.minimum(s+1,NS-1)
            @pl.when(s>=2)
            def _(): copy(s-2,buf).wait()
            for k in range(1,13):
                if k<12:
                    issue(accs,s,k,nxt)
                else:
                    issue(accs,nxt,0,nxt)
                c,p=divmod(k,3)
                if c>0 and p<2 and k<12: post(accs,s,c-1,p)
                if k==6: prep(nxt)
            post(accs,s,3,0)
            post(accs,s,3,1)
            copy(s,buf).start()
            return 0
        lax.fori_loop(0,NS,step,0)
        for mx in range(2):
            pltpu.matmul_acc_lhs(accs[mx][0][0],kt[:,mx*256:(mx+1)*256],load_staged_rhs=1)
        tot=jnp.zeros((64,256),F32)
        for mx in range(2):
            for i8 in range(I8):
                tot=tot+pltpu.matmul_pop(accs[mx][0][i8])
        ANG[0]=tot[0:32]
        copy(14,0).wait(); copy(15,1).wait()
    pl.run_scoped(whole,*[pltpu.ACC(mx)((64,256),F32) for mx in range(2) for _ in range(16)])

def gather(wave, labels, rows, cols, owners, kt):
    vm = pl.BlockSpec(memory_space=pltpu.VMEM)
    blocks = pltpu.VMEM((2, 4, 4, 4, 16, 128), BF)
    i32 = jnp.int32
    dma = pltpu.SemaphoreType.DMA
    return pl.pallas_call(
        gather_kernel,
        in_specs=[pl.BlockSpec(memory_space=pltpu.HBM)] * 6,
        out_specs=[vm] * 4,
        out_shape=[
            jax.ShapeDtypeStruct((49, 32, 512), BF),
            jax.ShapeDtypeStruct((RPT, NS, 128), F32),
            jax.ShapeDtypeStruct((2, 2, 4, 1, 128), i32),
            jax.ShapeDtypeStruct((D, 512), BF),
        ],
        scratch_shapes=[
            blocks, blocks, blocks,
            pltpu.VMEM((4, 4, 1, 128), i32),
            pltpu.VMEM((4, 4, 1, 128), i32),
            pltpu.VMEM((2, 4, 2, 1, 128), i32),
            pltpu.VMEM((64, 96), BF),
            pltpu.VMEM((1, 96), i32),
            pltpu.VMEM((1, 64), i32),
            pltpu.VMEM((1, 64), i32),
            pltpu.VMEM((1, 64), i32),
            dma((6,)),
            dma((3, 3)), dma((3, 4)), dma((3,)), dma((3, 3)), dma((3,)), dma((3,)),
        ],
        compiler_params=pltpu.CompilerParams(
            collective_id=0, has_side_effects=True, vmem_limit_bytes=24 * 2**20
        ),
    )(wave, labels, rows, cols, owners, kt)


def forms(meta, w_all, lt, kt):
    vm = pl.BlockSpec(memory_space=pltpu.VMEM)
    return pl.pallas_call(
        forms_kernel,
        in_specs=[pl.BlockSpec(memory_space=pltpu.SMEM), vm, vm, vm],
        out_specs=pl.BlockSpec(memory_space=pltpu.HBM),
        out_shape=jax.ShapeDtypeStruct((NS * CAP, D, 1024), BF),
        scratch_shapes=[
            pltpu.VMEM((2, CAP, D, 1024), BF),
            pltpu.VMEM((2, 32, 256), F32),
            pltpu.VMEM((RPT, 32, 128), F32),
            pltpu.SemaphoreType.DMA((2,)),
        ],
        compiler_params=pltpu.CompilerParams(vmem_limit_bytes=40 * 2**20),
    )(meta, w_all, lt, kt)


def per_device(wavefuncs, kernel, labels, row_tiles, col_tiles, owners):
    def in_hbm(v):
        return pltpu.with_memory_space_constraint(v, pltpu.HBM)

    w_all, lt, meta, kt = gather(
        in_hbm(wavefuncs.T),
        in_hbm(labels.reshape(1, 96)),
        in_hbm(row_tiles.reshape(1, 64)),
        in_hbm(col_tiles.reshape(1, 64)),
        in_hbm(owners.T),
        in_hbm(kernel.T),
    )
    return forms(meta.reshape(NS, 1, 128), w_all, lt, kt)


def solution(mesh):
    return jax.shard_map(
        per_device,
        mesh=mesh,
        in_specs=(P("bin", "dist"), P(None, "dist"), P("bin"), P("bin"), P("bin"), P("bin", None)),
        out_specs=P("bin", "dist", None),
        check_vma=False,
    )
```

time: 55.4 us -> 52.4 us (0.946)
  Pallas kernels: 55.2 us -> 52.3 us
    pallas_call x1, Pallas kernels: 23.1 us -> 21.3 us  [gather(): pl.pallas_call(gather_kernel, in_specs=[pl.BlockSpec(memory_space=pltpu.H...]
    pallas_call x1, Pallas kernels: 32.1 us -> 31 us  [forms(): pl.pallas_call(forms_kernel, in_specs=[pl.BlockSpec(memory_space=pltpu.SM...]
where the time goes in v3:
time: 52.4 us; the launch traced here: 52.3 us
  Pallas kernels  52.3 us (100%)
    pallas_call x1, Pallas kernels, forms(): pl.pallas_call(forms_kernel, in_specs=[pl.BlockSpec(memory_space=pltpu.SM...  31 us
    pallas_call x1, Pallas kernels, gather(): pl.pallas_call(gather_kernel, in_specs=[pl.BlockSpec(memory_space=pltpu.H...  21.3 us

profile of v3, /device:TPU:1, one launch (start us, length us, event | category | flops | bytes accessed | tf_op | source)
XLA Modules:
  0.0 52.3 jit_solution(11438505797946996568)
XLA Ops:
  0.0 21.3 %shard_map.64 = (bf16[49,32,512]{2,1,0:T(8,128)(2,1)S(1)}, f32[3,16,128]{2,1,0:T(8,128)S(1)}, s32[2,2,4,1,128]{4,3,2,1,0:T(1,128)S(1)}, bf16[64,512]{1,0:T(8,128)(2,1)S(1)}) custom-call(bf16[64,96]{1,0:T(8,128)(2,1)} %bitcast.9, s32[1,96]{1,0:T(1,128)} %bitcast.10, s32[1,64]{1,0:T(1,128)} %bitcast.11, s32[1,64]{1,0:T(1,128)} %bitcast.12, s32[1,64]{1,0:T(1,128)} %bitcast.13, ...), custom_call_target="tpu_custom_call" | custom-call | tf_op jit(solution)/shard_map/pallas_call | solution.py:347
  21.3 31.0 %shard_map.65 = bf16[128,64,1024]{2,1,0:T(8,128)(2,1)} custom-call(s32[16,1,128]{2,1,0:T(1,128)S(1)} %bitcast.7, bf16[49,32,512]{2,1,0:T(8,128)(2,1)S(1)} %get-tuple-element.10.W, f32[3,16,128]{2,1,0:T(8,128)S(1)} %get-tuple-element.11.LT, bf16[64,512]{1,0:T(8,128)(2,1)S(1)} %get-tuple-element.12.kt_ref), custom_call_target="tpu_custom_call" | custom-call | tf_op jit(solution)/shard_map/pallas_call | solution.py:378

commit v4 on v3

--- a/solution.py
+++ b/solution.py
@@ -15,8 +15,78 @@
 MESH = pl.DeviceIdType.MESH
 
 
-def gather_kernel(wave_in, labels_in, rows_in, cols_in, owners_in, kt_in, w_all, lt, meta, kt,
-                  b0, b1, b2, table, via_x, via_y, wave, labels, rows, cols, owners, in_sem,
+TILES, DEST, ROW, PAIR, PAIR_TILE = 0, 16, 24, 27, 29
+
+
+def factor(li, lj):
+    return jnp.sqrt((2.0 * li + 1.0) * (2.0 * lj + 1.0)) / (8.0 * (1.0 + jnp.abs(li - lj)))
+
+
+def tables(meta, roles, ang, ang_pair):
+    lane = lax.broadcasted_iota(jnp.int32, (NS, 128), 1)
+    sender = lax.broadcasted_iota(jnp.int32, (NS, 128), 0)
+    found = jnp.concatenate([meta[c, h, p] for c in range(2) for h in range(2) for p in range(4)], axis=0)
+    ok = (found > 0) & (lane < CAP)
+    at = jnp.maximum(found - 1, 0)
+    row, tile = at >> 6, at & 63
+
+    def total(mask, value):
+        return jnp.sum(jnp.where(mask, value, 0), axis=1, keepdims=True)
+
+    n = [total(ok & (row == r), 1) for r in range(RPT)]
+    third = jnp.where((n[0] <= n[1]) & (n[0] <= n[2]), 0, jnp.where(n[1] <= n[2], 1, 2))
+    first = jnp.where(third == 0, 1, 0)
+    second = jnp.where(third == 2, 1, 2)
+    single = ok & (row == third)
+    p0 = jnp.min(jnp.where(single, lane, CAP), axis=1, keepdims=True)
+    p1 = jnp.max(jnp.where(single, lane, -1), axis=1, keepdims=True)
+    p1 = jnp.where((p1 == p0) | (p1 < 0), CAP, p1)
+    t0 = jnp.where(p0 < CAP, total(single & (lane == p0), tile), 48)
+    t1 = jnp.where(p1 < CAP, total(single & (lane == p1), tile), 48)
+    role = jnp.where(ok & (row == first), tile, 48)
+    role = jnp.where(lane < 8, role, pltpu.roll(jnp.where(ok & (row == second), tile, 48), 8, 1))
+    role = jnp.where(lane < 16, role, pltpu.roll(jnp.where(single, CAP, lane), 16, 1))
+    for k, v in enumerate((first * 16 + sender, second * 16 + sender, third * 16 + sender, p0, p1, t0, t1)):
+        role = jnp.where(lane == ROW + k, v, role)
+    for s in range(NS):
+        roles[s] = role[s : s + 1, :]
+
+    real = found.astype(F32)
+    rolled = [real] + [pltpu.roll(real, 32 * k, 1) for k in (1, 2, 3)]
+    labels = []
+    for rt in range(RPT):
+        v = rolled[(0 - rt - 1) % 4]
+        for g in (1, 2, 3):
+            v = jnp.where(lane // 32 == g, rolled[(g - rt - 1) % 4], v)
+        labels.append(v)
+    row_of = [jnp.take_along_axis(row, lane // 32 + 4 * h, axis=1) for h in range(2)]
+    tile_of = [jnp.take_along_axis(tile, lane // 32 + 4 * h, axis=1) for h in range(2)]
+    tile_of += [jnp.broadcast_to(t, (NS, 128)) for t in (t0, t1)]
+    col = [jnp.zeros((NS, 128), F32) for _ in tile_of]
+    for t in range(48):
+        of = jnp.broadcast_to(labels[t // 16][t % 16 : t % 16 + 1, :], (NS, 128))
+        col = [jnp.where(which == t, of, v) for which, v in zip(tile_of, col)]
+    of_third = jnp.where(third == 0, labels[0], jnp.where(third == 1, labels[1], labels[2]))
+    lane32 = lax.broadcasted_iota(jnp.int32, (32, 128), 1)
+    eye = lane32 == lax.broadcasted_iota(jnp.int32, (32, 128), 0)
+    spread = lax.broadcasted_iota(jnp.int32, (8, 128), 0) * 4 + lax.broadcasted_iota(jnp.int32, (8, 128), 1) // 32
+
+    def line(v, s, rows):
+        return jnp.broadcast_to(v[s : s + 1, :], (rows, 128))
+
+    for s in range(NS):
+        down = [jnp.sum(jnp.where(eye, line(labels[rt], s, 32), 0.0), axis=1, keepdims=True) for rt in range(RPT)]
+        for h in range(2):
+            r = line(row_of[h], s, 32)
+            li = jnp.where(r == 0, down[0], jnp.where(r == 1, down[1], down[2]))
+            ang[s, :, h * 128 : (h + 1) * 128] = factor(li, line(col[h], s, 32))
+        li = jnp.take_along_axis(line(of_third, s, 8), spread, axis=1)
+        for e in range(2):
+            ang_pair[s, e] = factor(li, line(col[2 + e], s, 8))
+
+
+def gather_kernel(wave_in, labels_in, rows_in, cols_in, owners_in, kt_in, w_all, roles, ang, ang_pair, kt,
+                  b0, b1, b2, meta, table, via_x, via_y, wave, labels, rows, cols, owners, in_sem,
                   z_send, z_recv, c_send, c_recv, m_send, m_recv):
     loads = [
         pltpu.make_async_copy(src, dst, in_sem.at[k])
@@ -185,15 +255,7 @@
 
     arrived(meta.at[other], m_recv.at[2])
     meta_c.wait_send()
-    lane16 = lax.broadcasted_iota(jnp.int32, (NS, 128), 1)
-    found = jnp.concatenate([meta[c, h, p] for c in range(2) for h in range(2) for p in range(4)], axis=0)
-    found = found.astype(F32)
-    rolled = [found] + [pltpu.roll(found, 32 * k, 1) for k in (1, 2, 3)]
-    for rt in range(RPT):
-        labs = rolled[(0 - rt - 1) % 4]
-        for g in (1, 2, 3):
-            labs = jnp.where(lane16 // 32 == g, rolled[(g - rt - 1) % 4], labs)
-        lt[rt] = labs
+    tables(meta, roles, ang, ang_pair)
     for rt in range(RPT):
         arrived(some(rt, 2, 2), z_recv.at[rt, 2])
         across(rt, 1, 1)
@@ -225,119 +287,166 @@
 
 
 def swap_blocks(lane, x):
-    half=lane<64
-    even=(lane//32)%2==0
-    def cross(p,q,shift,mask):
-        return jnp.where(mask,p,pltpu.roll(q,shift,1)), jnp.where(mask,pltpu.roll(p,128-shift,1),q)
-    a0,a2=cross(x[0],x[2],64,half)
-    a1,a3=cross(x[1],x[3],64,half)
-    y0,y1=cross(a0,a1,32,even)
-    y2,y3=cross(a2,a3,32,even)
-    return y0,y1,y2,y3
-
-def forms_kernel(msm, W, LT, kt_ref, out, OUT, ANG, LC, sem):
-    lane=lax.broadcasted_iota(jnp.int32,(64,128),1)
-    eye=(lax.broadcasted_iota(jnp.int32,(32,128),1)==lax.broadcasted_iota(jnp.int32,(32,128),0))
-    blk=lax.broadcasted_iota(jnp.int32,(32,128),1)//32
-    kt=kt_ref[...]
-    I8=8
-
-    def codes(s):
-        out=[]
-        for n in range(CAP):
-            code=msm[s,0,n]
-            cm=jnp.maximum(code-1,0)
-            out.append((code>0,cm>>6,cm&63))
-        return out
-
-    def prep(s):
-        cs=codes(s)
-        for rt in range(RPT):
-            lrow=LT[rt,pl.ds(s,1),:]
-            li=jnp.sum(jnp.where(eye,jnp.broadcast_to(lrow,(32,128)),0.0),axis=1,keepdims=True)
-            LC[rt]=jnp.broadcast_to(li,(32,128))
-        for h in range(2):
-            lj=li=None
-            for g in range(4):
-                _,rt,t=cs[h*4+g]
-                row=jnp.broadcast_to(LT[t>>4,pl.ds(t&15,1),:],(32,128))
-                col=LC[rt]
-                lj=row if lj is None else jnp.where(blk==g,row,lj)
-                li=col if li is None else jnp.where(blk==g,col,li)
-            ANG[lax.rem(s,2),:,h*128:(h+1)*128]=jnp.sqrt((2.0*li+1.0)*(2.0*lj+1.0))/(8.0*(1.0+jnp.abs(li-lj)))
-
-    def rt_of(k):
-        c,p=divmod(k%12,3)
-        return p if c%2==0 else 2-p
-    fresh=[k for k in range(12) if k==0 or rt_of(k)!=rt_of(k-1)]
-    def push(s,k):
-        rt=rt_of(k)
-        tiles=[W[jnp.where(ok&(r==rt),t,48)] for ok,r,t in codes(s)]
-        cols=jnp.concatenate(tiles,axis=0)
-        for mx in range(2):
-            pltpu.matmul_push_rhs(cols[:,mx*256:(mx+1)*256],fresh.index(k)%2,mx,transpose=True)
-
-    def issue(accs,s,k,snext):
-        c=k//3
-        rt=rt_of(k)
-        for i8 in range(I8):
-            i=c*I8+i8
-            lhs=W[rt*16+s,i:i+1,:]*kt
-            for mx in range(2):
-                pltpu.matmul_acc_lhs(accs[mx][c%2][i8],lhs[:,mx*256:(mx+1)*256],load_staged_rhs=(fresh.index(k)%2) if i8==0 and k in fresh else None)
-            if i8==0 and k in fresh:
-                j=fresh.index(k)+1
-                push(s if j<len(fresh) else snext,fresh[j%len(fresh)])
-
-    def post(accs,s,c,half):
-        buf=lax.rem(s,2)
-        lows,highs=[],[]
-        for i4 in range(4):
-            i8=half*4+i4
-            i=c*I8+i8
-            f=(pltpu.matmul_pop(accs[0][c%2][i8])+pltpu.matmul_pop(accs[1][c%2][i8]))*ANG[buf,i:i+1,:]
-            f=f.astype(BF)
-            lows.append(f[:,:128]); highs.append(f[:,128:])
-        q=c*2+half
-        for base,xs in ((0,lows),(4,highs)):
-            for n,v in enumerate(swap_blocks(lane,xs)):
-                OUT[buf,base+n,:,q*128:(q+1)*128]=v
+    half, even = lane
+
+    def mixed(a, b, c, d):
+        ab, cd = jnp.where(even, a, b), jnp.where(even, c, d)
+        return jnp.where(half, ab, cd), jnp.where(half, cd, ab)
+
+    z0, z2 = mixed(x[0], x[1], x[2], x[3])
+    z1, z3 = mixed(x[3], x[0], x[1], x[2])
+    u = z0, pltpu.roll(z1, 96, 1), pltpu.roll(z2, 64, 1), pltpu.roll(z3, 32, 1)
+    y0, y2 = mixed(u[0], u[3], u[2], u[1])
+    y1, y3 = mixed(u[1], u[0], u[3], u[2])
+    return y0, y1, y2, y3
+
+
+CHUNKS = ((0, 6), (6, 12), (12, 17), (17, 22), (22, 27), (27, 32))
+STEPS = ((0, 0), 0, (0, 1), (1, 1), 1, (1, 0), 2, (2, 0), 3, (2, 1), (3, 1), 4, (3, 0), 5, (4, 0), 6, (4, 1), (5, 1), 7, (5, 0))
+
+
+def loads_weights(k):
+    return isinstance(STEPS[k], int) or isinstance(STEPS[k - 1], int) or k == 0 or STEPS[k][1] != STEPS[k - 1][1]
+
+
+WIDE = [k for k, step in enumerate(STEPS) if not isinstance(step, int) and loads_weights(k)]
+
+
+def forms_kernel(roles, W, ANG, ANGP, kt_ref, out, OUT, cols_first, cols_second, sem):
+    place = lax.broadcasted_iota(jnp.int32, (16, 128), 1) // 32
+    lane_f = (place // 2).astype(F32).astype(BF), (place % 2).astype(F32).astype(BF)
+    def halves(m):
+        return slice(m * 256, (m + 1) * 256)
+
+    def turn(s, which):
+        cols = jnp.concatenate([W[roles[s, 0, TILES + 8 * which + n]] for n in range(CAP)], axis=0)
+        (cols_first, cols_second)[which][...] = cols.T
+
+    def push_wide(which):
+        cols = (cols_first, cols_second)[which]
+        for m in range(2):
+            pltpu.matmul_push_rhs(cols[halves(m), :], 0, m)
+
+    def push_pair(s, j):
+        e, u, kh = j // 4, (j // 2) % 2, j % 2
+        rows = W.at[roles[s, 0, ROW + 2]]
+        cols = W[roles[s, 0, PAIR_TILE + e], :, halves(kh)]
+        for m in range(2):
+            at = (u * 2 + m) * 8
+            pair = jnp.concatenate([rows[i : i + 1, halves(kh)] * cols for i in range(at, at + 8)], axis=0)
+            pltpu.matmul_push_rhs(pair, 1, m, transpose=True)
 
     def whole(*flat):
-        accs=[[flat[mx*16+b*8:mx*16+b*8+8] for b in range(2)] for mx in range(2)]
-        def copy(s,buf):
-            place=(s%4)*4+((s//4)%2)*2+s//8
-            return pltpu.make_async_copy(OUT.at[buf],out.at[pl.ds(place*8,8)],sem.at[buf])
-        prep(0)
-        push(0,0)
-        issue(accs,0,0,0)
-        def step(s,_):
-            buf=lax.rem(s,2)
-            nxt=jnp.minimum(s+1,NS-1)
-            @pl.when(s>=2)
-            def _(): copy(s-2,buf).wait()
-            for k in range(1,13):
-                if k<12:
-                    issue(accs,s,k,nxt)
+        wide = [[flat[m * 16 + b * 6 : m * 16 + b * 6 + 6] for b in range(2)] for m in range(2)]
+        narrow = [flat[m * 16 + 12 : m * 16 + 16] for m in range(2)]
+
+        def step(s, k, nxt):
+            what = STEPS[k]
+            if isinstance(what, int):
+                kh = what % 2
+                for m in range(2):
+                    pltpu.matmul_acc_lhs(narrow[m][what // 2], kt_ref[:, halves(kh)], load_staged_rhs=1)
+                push_pair(s if what < 7 else nxt, (what + 1) % 8)
+                return
+            c, which = what
+            row = roles[s, 0, ROW + which]
+            lo, hi = CHUNKS[c]
+            for u in range(lo, hi):
+                g, db = u // 4, u % 4
+                kt = kt_ref[db * 16 : (db + 1) * 16, :]
+                if u == lo or db == 0:
+                    wide_rows = [jnp.broadcast_to(W[row, i : i + 1, :], (16, 512)) for i in range(g * 4, g * 4 + 4)]
+                lhs = jnp.concatenate([r * kt for r in wide_rows], axis=0)
+                load = u == lo and loads_weights(k)
+                for m in range(2):
+                    pltpu.matmul_acc_lhs(wide[m][c % 2][u - lo], lhs[:, halves(m)], load_staged_rhs=0 if load else None)
+                if load:
+                    at = WIDE.index(k) + 1
+                    if at == len(WIDE):
+                        turn(nxt, 0)
+                    push_wide(STEPS[WIDE[at % len(WIDE)]][1])
+                    if at == len(WIDE) - 1:
+                        turn(nxt, 1)
+
+        def post_wide(s, c, part, dest):
+            buf = s % 2
+            lo, hi = CHUNKS[c]
+            mid = lo + (hi - lo + 1) // 2
+            for u in range(lo, mid) if part == 0 else range(mid, hi):
+                g, db = u // 4, u % 4
+                f = pltpu.matmul_pop(wide[0][c % 2][u - lo]) + pltpu.matmul_pop(wide[1][c % 2][u - lo])
+                low, high = [], []
+                for i4 in range(4):
+                    i = g * 4 + i4
+                    v = (f[i4 * 16 : (i4 + 1) * 16, :] * ANG[s, i : i + 1, :]).astype(BF)
+                    low.append(v[:, :128])
+                    high.append(v[:, 128:])
+                for base, xs in ((0, low), (4, high)):
+                    for n, v in enumerate(swap_blocks((lane_f[0] < 0.5, lane_f[1] < 0.5), xs)):
+                        OUT[buf, dest[base + n], db * 16 : (db + 1) * 16, g * 128 : (g + 1) * 128] = v
+
+        def post_pair(s, j):
+            buf = s % 2
+            e, u = j // 4, (j // 2) % 2
+            for m in range(2):
+                nt = u * 2 + m
+                f = pltpu.matmul_pop(narrow[m][j // 2])
+                for h in range(2):
+                    g = nt * 2 + h
+                    v = f[:, h * 128 : (h + 1) * 128] * ANGP[s, e, g : g + 1, :]
+                    OUT[buf, roles[s, 0, PAIR + e], :, g * 128 : (g + 1) * 128] = v.astype(BF)
+
+        def copy(s):
+            place = (s % 4) * 4 + ((s // 4) % 2) * 2 + s // 8
+            return pltpu.make_async_copy(OUT.at[s % 2, pl.ds(0, CAP)], out.at[pl.ds(place * CAP, CAP)], sem.at[s % 2])
+
+        turn(0, 0)
+        turn(0, 1)
+        push_wide(0)
+        push_pair(0, 0)
+        step(0, 0, 0)
+
+        def sender(s, _):
+            nxt = jnp.minimum(s + 1, NS - 1)
+            dest = [roles[s, 0, DEST + n] for n in range(CAP)]
+
+            @pl.when(s >= 2)
+            def _():
+                copy(s - 2).wait()
+
+            for k in range(1, len(STEPS) + 1):
+                if k < len(STEPS):
+                    step(s, k, nxt)
+                    what = STEPS[k]
                 else:
-                    issue(accs,nxt,0,nxt)
-                c,p=divmod(k,3)
-                if c>0 and p<2 and k<12: post(accs,s,c-1,p)
-                if k==6: prep(nxt)
-            post(accs,s,3,0)
-            post(accs,s,3,1)
-            copy(s,buf).start()
+                    step(nxt, 0, nxt)
+                    what = (6, 0)
+                if isinstance(what, int):
+                    continue
+                done = STEPS[k - 1]
+                if isinstance(done, int) and done % 2 == 1 and k < len(STEPS):
+                    post_pair(s, done)
+                c = what[0]
+                if c > 0:
+                    first = not any(not isinstance(w, int) and w[0] == c for w in STEPS[:k])
+                    post_wide(s, c - 1, 0 if first else 1, dest)
+            post_wide(s, 5, 1, dest)
+            copy(s).start()
             return 0
-        lax.fori_loop(0,NS,step,0)
-        for mx in range(2):
-            pltpu.matmul_acc_lhs(accs[mx][0][0],kt[:,mx*256:(mx+1)*256],load_staged_rhs=1)
-        tot=jnp.zeros((64,256),F32)
-        for mx in range(2):
-            for i8 in range(I8):
-                tot=tot+pltpu.matmul_pop(accs[mx][0][i8])
-        ANG[0]=tot[0:32]
-        copy(14,0).wait(); copy(15,1).wait()
-    pl.run_scoped(whole,*[pltpu.ACC(mx)((64,256),F32) for mx in range(2) for _ in range(16)])
+
+        lax.fori_loop(0, NS, sender, 0)
+        left = jnp.zeros((64, 256), F32)
+        for m in range(2):
+            pltpu.matmul_acc_lhs(wide[m][0][0], kt_ref[:, halves(m)], load_staged_rhs=0)
+            pltpu.matmul_acc_lhs(narrow[m][0], kt_ref[:, halves(m)], load_staged_rhs=1)
+            for acc in (*wide[m][0], narrow[m][0]):
+                left = left + pltpu.matmul_pop(acc)
+        OUT[0, CAP, :, 0:256] = left.astype(BF)
+        copy(NS - 2).wait()
+        copy(NS - 1).wait()
+
+    pl.run_scoped(whole, *[pltpu.ACC(m)((64, 256), F32) for m in range(2) for _ in range(16)])
+
 
 def gather(wave, labels, rows, cols, owners, kt):
     vm = pl.BlockSpec(memory_space=pltpu.VMEM)
@@ -347,15 +456,17 @@
     return pl.pallas_call(
         gather_kernel,
         in_specs=[pl.BlockSpec(memory_space=pltpu.HBM)] * 6,
-        out_specs=[vm] * 4,
+        out_specs=[vm] * 5,
         out_shape=[
             jax.ShapeDtypeStruct((49, 32, 512), BF),
-            jax.ShapeDtypeStruct((RPT, NS, 128), F32),
-            jax.ShapeDtypeStruct((2, 2, 4, 1, 128), i32),
+            jax.ShapeDtypeStruct((NS, 1, 128), i32),
+            jax.ShapeDtypeStruct((NS, 32, 256), F32),
+            jax.ShapeDtypeStruct((NS, 2, 8, 128), F32),
             jax.ShapeDtypeStruct((D, 512), BF),
         ],
         scratch_shapes=[
             blocks, blocks, blocks,
+            pltpu.VMEM((2, 2, 4, 1, 128), i32),
             pltpu.VMEM((4, 4, 1, 128), i32),
             pltpu.VMEM((4, 4, 1, 128), i32),
             pltpu.VMEM((2, 4, 2, 1, 128), i32),
@@ -373,28 +484,28 @@
     )(wave, labels, rows, cols, owners, kt)
 
 
-def forms(meta, w_all, lt, kt):
+def forms(roles, w_all, ang, ang_pair, kt):
     vm = pl.BlockSpec(memory_space=pltpu.VMEM)
     return pl.pallas_call(
         forms_kernel,
-        in_specs=[pl.BlockSpec(memory_space=pltpu.SMEM), vm, vm, vm],
+        in_specs=[pl.BlockSpec(memory_space=pltpu.SMEM), vm, vm, vm, vm],
         out_specs=pl.BlockSpec(memory_space=pltpu.HBM),
         out_shape=jax.ShapeDtypeStruct((NS * CAP, D, 1024), BF),
         scratch_shapes=[
-            pltpu.VMEM((2, CAP, D, 1024), BF),
-            pltpu.VMEM((2, 32, 256), F32),
-            pltpu.VMEM((RPT, 32, 128), F32),
+            pltpu.VMEM((2, CAP + 1, D, 1024), BF),
+            pltpu.VMEM((512, 256), BF),
+            pltpu.VMEM((512, 256), BF),
             pltpu.SemaphoreType.DMA((2,)),
         ],
         compiler_params=pltpu.CompilerParams(vmem_limit_bytes=40 * 2**20),
-    )(meta, w_all, lt, kt)
+    )(roles, w_all, ang, ang_pair, kt)
 
 
 def per_device(wavefuncs, kernel, labels, row_tiles, col_tiles, owners):
     def in_hbm(v):
         return pltpu.with_memory_space_constraint(v, pltpu.HBM)
 
-    w_all, lt, meta, kt = gather(
+    w_all, roles, ang, ang_pair, kt = gather(
         in_hbm(wavefuncs.T),
         in_hbm(labels.reshape(1, 96)),
         in_hbm(row_tiles.reshape(1, 64)),
@@ -402,7 +513,7 @@
         in_hbm(owners.T),
         in_hbm(kernel.T),
     )
-    return forms(meta.reshape(NS, 1, 128), w_all, lt, kt)
+    return forms(roles, w_all, ang, ang_pair, kt)
 
 
 def solution(mesh):

time: 52.4 us -> 48.8 us (0.931)
  Pallas kernels: 52.3 us -> 48.7 us
    pallas_call x1, Pallas kernels: 31 us -> 27.4 us  [forms(): pl.pallas_call(forms_kernel, in_specs=[pl.BlockSpec(memory_space=pltpu.SM...]
where the time goes in v4:
time: 48.8 us; the launch traced here: 48.7 us
  Pallas kernels  48.7 us (100%)
    pallas_call x1, Pallas kernels, forms(): pl.pallas_call(forms_kernel, in_specs=[pl.BlockSpec(memory_space=pltpu.SM...  27.4 us
    pallas_call x1, Pallas kernels, gather(): pl.pallas_call(gather_kernel, in_specs=[pl.BlockSpec(memory_space=pltpu.H...  21.3 us

profile of v4, /device:TPU:1, one launch (start us, length us, event | category | flops | bytes accessed | tf_op | source)
XLA Modules:
  0.0 48.7 jit_solution(9305389978989080615)
XLA Ops:
  0.0 21.3 %shard_map.64 = (bf16[49,32,512]{2,1,0:T(8,128)(2,1)S(1)}, s32[16,1,128]{2,1,0:T(1,128)S(1)}, f32[16,32,256]{2,1,0:T(8,128)S(1)}, f32[16,2,8,128]{3,2,1,0:T(8,128)S(1)}, bf16[64,512]{1,0:T(8,128)(2,1)S(1)}) custom-call(bf16[64,96]{1,0:T(8,128)(2,1)} %bitcast.7, s32[1,96]{1,0:T(1,128)} %bitcast.8, s32[1,64]{1,0:T(1,128)} %bitcast.9, s32[1,64]{1,0:T(1,128)} %bitcast.10, ...), custom_call_target="tpu_custom_call" | custom-call | tf_op jit(solution)/shard_map/pallas_call | solution.py:456
  21.3 27.4 %shard_map.65 = bf16[128,64,1024]{2,1,0:T(8,128)(2,1)} custom-call(s32[16,1,128]{2,1,0:T(1,128)S(1)} %get-tuple-element.10.roles, bf16[49,32,512]{2,1,0:T(8,128)(2,1)S(1)} %get-tuple-element.11.W, f32[16,32,256]{2,1,0:T(8,128)S(1)} %get-tuple-element.12.ANG, f32[16,2,8,128]{3,2,1,0:T(8,128)S(1)} %get-tuple-element.13.ANGP, ...), custom_call_target="tpu_custom_call" | custom-call | tf_op jit(solution)/shard_map/pallas_call | solution.py:489

commit v5 on v4

--- a/solution.py
+++ b/solution.py
@@ -113,8 +113,13 @@
             up(x, o) if axis == "x" else x, up(y, o) if axis == "y" else y, up(z, o) if axis == "z" else z, core
         )
 
+    def diagonal(axis, o, axis2, o2):
+        by = {axis: o, axis2: o2}
+        return chip(up(x, by.get("x", 0)), up(y, by.get("y", 0)), up(z, by.get("z", 0)), core)
+
     barrier = pltpu.get_barrier_semaphore()
     peers = [peer(axis, o) for o in (2, 1, 3) for axis in "xyz"] + [chip(x, y, z, other)]
+    peers += [diagonal(p, o, q, o2) for p, q in ("zy", "yx", "xz") for o in (2, 1, 3) for o2 in (2, 1, 3)]
     for at in peers:
         pl.semaphore_signal(barrier, inc=1, device_id=at, device_id_type=MESH)
 
@@ -194,8 +199,10 @@
                 for px in range(4):
                     lay(2, c, px, v, pz, b2[c, 2 * v, pz, px], b2[c, 2 * v + 1, pz, px])
 
-    for rt in range(RPT):
-        push(rt, 0)
+    for o, o2 in [(a, b) for a in (2, 1, 3, 0) for b in (2, 1, 3, 0) if a or b]:
+        for rt, (p, q) in enumerate(("zy", "yx", "xz")):
+            mine = block(rt, 0, place(rt, 0)[0], core)
+            copy(mine, mine, z_send.at[rt, 0], z_recv.at[rt, 1 if o2 else 0], diagonal(p, o, q, o2)).start()
 
     for load in loads[1:]:
         load.wait()
@@ -224,11 +231,6 @@
         copy(table.at[up(x, o)], via_x.at[x], m_send.at[0], m_recv.at[0], peer("x", o)).start()
     via_x[x] = table[x]
 
-    for rt in range(RPT):
-        arrived(some(rt, 0, 3), z_recv.at[rt, 0])
-        push(rt, 1)
-    for rt in range(RPT):
-        taken(some(rt, 0, 3), z_send.at[rt, 0])
 
     arrived(via_x.at[pl.ds(0, 3)], m_recv.at[0])
     taken(table.at[pl.ds(0, 3)], m_send.at[0])
@@ -238,11 +240,13 @@
     via_y[yh] = via_x[:, pl.ds(yh * 2, 2)]
 
     for rt in range(RPT):
+        arrived(some(rt, 0, 3), z_recv.at[rt, 0])
         arrived(some(rt, 1, 3), z_recv.at[rt, 1])
         push(rt, 2)
         across(rt, 0, 0)
     for rt in range(RPT):
-        taken(some(rt, 1, 3), z_send.at[rt, 1])
+        taken(some(rt, 0, 3), z_send.at[rt, 0])
+        taken(some(rt, 1, 3), z_send.at[rt, 0])
 
     arrived(via_y.at[far], m_recv.at[1])
     meta_c = copy(via_y.at[:, :, other], meta.at[core], m_send.at[2], m_recv.at[2], chip(x, y, z, other))

time: 48.8 us -> 48.4 us (level)
  Pallas kernels: 48.7 us -> 48.2 us
where the time goes in v5:
time: 48.4 us; the launch traced here: 48.2 us
  Pallas kernels  48.2 us (100%)
    pallas_call x1, Pallas kernels, forms(): pl.pallas_call(forms_kernel, in_specs=[pl.BlockSpec(memory_space=pltpu.SM...  27.4 us
    pallas_call x1, Pallas kernels, gather(): pl.pallas_call(gather_kernel, in_specs=[pl.BlockSpec(memory_space=pltpu.H...  20.8 us

profile of v5, /device:TPU:1, one launch (start us, length us, event | category | flops | bytes accessed | tf_op | source)
XLA Modules:
  0.0 48.2 jit_solution(6470240341618302762)
XLA Ops:
  0.0 20.8 %shard_map.64 = (bf16[49,32,512]{2,1,0:T(8,128)(2,1)S(1)}, s32[16,1,128]{2,1,0:T(1,128)S(1)}, f32[16,32,256]{2,1,0:T(8,128)S(1)}, f32[16,2,8,128]{3,2,1,0:T(8,128)S(1)}, bf16[64,512]{1,0:T(8,128)(2,1)S(1)}) custom-call(bf16[64,96]{1,0:T(8,128)(2,1)} %bitcast.7, s32[1,96]{1,0:T(1,128)} %bitcast.8, s32[1,64]{1,0:T(1,128)} %bitcast.9, s32[1,64]{1,0:T(1,128)} %bitcast.10, ...), custom_call_target="tpu_custom_call" | custom-call | tf_op jit(solution)/shard_map/pallas_call | solution.py:460
  20.8 27.4 %shard_map.65 = bf16[128,64,1024]{2,1,0:T(8,128)(2,1)} custom-call(s32[16,1,128]{2,1,0:T(1,128)S(1)} %get-tuple-element.10.roles, bf16[49,32,512]{2,1,0:T(8,128)(2,1)S(1)} %get-tuple-element.11.W, f32[16,32,256]{2,1,0:T(8,128)S(1)} %get-tuple-element.12.ANG, f32[16,2,8,128]{3,2,1,0:T(8,128)S(1)} %get-tuple-element.13.ANGP, ...), custom_call_target="tpu_custom_call" | custom-call | tf_op jit(solution)/shard_map/pallas_call | solution.py:493

commit v6 on v5

--- a/solution.py
+++ b/solution.py
@@ -305,12 +305,19 @@
     return y0, y1, y2, y3
 
 
-CHUNKS = ((0, 6), (6, 12), (12, 17), (17, 22), (22, 27), (27, 32))
-STEPS = ((0, 0), 0, (0, 1), (1, 1), 1, (1, 0), 2, (2, 0), 3, (2, 1), (3, 1), 4, (3, 0), 5, (4, 0), 6, (4, 1), (5, 1), 7, (5, 0))
+CHUNKS = ((0, 6), (6, 12), (12, 16))
+WEIGHTS = ((0, 0), (0, 1), (1, 0), (1, 1))
+STEPS = []
+for c, order in enumerate((WEIGHTS, WEIGHTS[::-1], WEIGHTS)):
+    for n, weights in enumerate(order):
+        STEPS.append((c, *weights))
+        piece = c * 3 + n
+        if n < 3 and piece < 8:
+            STEPS.append(piece)
 
 
 def loads_weights(k):
-    return isinstance(STEPS[k], int) or isinstance(STEPS[k - 1], int) or k == 0 or STEPS[k][1] != STEPS[k - 1][1]
+    return k == 0 or isinstance(STEPS[k], int) or isinstance(STEPS[k - 1], int) or STEPS[k][1:] != STEPS[k - 1][1:]
 
 
 WIDE = [k for k, step in enumerate(STEPS) if not isinstance(step, int) and loads_weights(k)]
@@ -326,10 +333,9 @@
         cols = jnp.concatenate([W[roles[s, 0, TILES + 8 * which + n]] for n in range(CAP)], axis=0)
         (cols_first, cols_second)[which][...] = cols.T
 
-    def push_wide(which):
-        cols = (cols_first, cols_second)[which]
+    def push_wide(which, kh):
         for m in range(2):
-            pltpu.matmul_push_rhs(cols[halves(m), :], 0, m)
+            pltpu.matmul_push_rhs((cols_first, cols_second)[which][halves(kh), :], 0, m)
 
     def push_pair(s, j):
         e, u, kh = j // 4, (j // 2) % 2, j % 2
@@ -344,7 +350,7 @@
         wide = [[flat[m * 16 + b * 6 : m * 16 + b * 6 + 6] for b in range(2)] for m in range(2)]
         narrow = [flat[m * 16 + 12 : m * 16 + 16] for m in range(2)]
 
-        def step(s, k, nxt):
+        def step(s, buf, k, nxt):
             what = STEPS[k]
             if isinstance(what, int):
                 kh = what % 2
@@ -352,45 +358,47 @@
                     pltpu.matmul_acc_lhs(narrow[m][what // 2], kt_ref[:, halves(kh)], load_staged_rhs=1)
                 push_pair(s if what < 7 else nxt, (what + 1) % 8)
                 return
-            c, which = what
+            c, which, kh = what
             row = roles[s, 0, ROW + which]
             lo, hi = CHUNKS[c]
-            for u in range(lo, hi):
-                g, db = u // 4, u % 4
-                kt = kt_ref[db * 16 : (db + 1) * 16, :]
-                if u == lo or db == 0:
-                    wide_rows = [jnp.broadcast_to(W[row, i : i + 1, :], (16, 512)) for i in range(g * 4, g * 4 + 4)]
-                lhs = jnp.concatenate([r * kt for r in wide_rows], axis=0)
-                load = u == lo and loads_weights(k)
+            for v in range(lo, hi):
+                g = v // 2
+                if v == lo or v % 2 == 0:
+                    wide_rows = [
+                        jnp.broadcast_to(W[row, i : i + 1, halves(kh)], (16, 256)) for i in range(g * 4, g * 4 + 4)
+                    ]
+                load = v == lo and loads_weights(k)
                 for m in range(2):
-                    pltpu.matmul_acc_lhs(wide[m][c % 2][u - lo], lhs[:, halves(m)], load_staged_rhs=0 if load else None)
+                    db = 2 * m + v % 2
+                    kt = kt_ref[db * 16 : (db + 1) * 16, halves(kh)]
+                    lhs = jnp.concatenate([r * kt for r in wide_rows], axis=0)
+                    acc = wide[m][(3 * buf + c) % 2][v - lo]
+                    pltpu.matmul_acc_lhs(acc, lhs, load_staged_rhs=0 if load else None)
                 if load:
                     at = WIDE.index(k) + 1
-                    if at == len(WIDE):
-                        turn(nxt, 0)
-                    push_wide(STEPS[WIDE[at % len(WIDE)]][1])
-                    if at == len(WIDE) - 1:
-                        turn(nxt, 1)
-
-        def post_wide(s, c, part, dest):
-            buf = s % 2
+                    coming = STEPS[WIDE[at % len(WIDE)]][1:]
+                    push_wide(*coming)
+                    if at < len(WIDE) and not any(STEPS[j][1] == coming[0] for j in WIDE[at + 1 :]):
+                        turn(nxt, coming[0])
+
+        def post_wide(s, buf, c, part, dest):
             lo, hi = CHUNKS[c]
             mid = lo + (hi - lo + 1) // 2
-            for u in range(lo, mid) if part == 0 else range(mid, hi):
-                g, db = u // 4, u % 4
-                f = pltpu.matmul_pop(wide[0][c % 2][u - lo]) + pltpu.matmul_pop(wide[1][c % 2][u - lo])
-                low, high = [], []
-                for i4 in range(4):
-                    i = g * 4 + i4
-                    v = (f[i4 * 16 : (i4 + 1) * 16, :] * ANG[s, i : i + 1, :]).astype(BF)
-                    low.append(v[:, :128])
-                    high.append(v[:, 128:])
-                for base, xs in ((0, low), (4, high)):
-                    for n, v in enumerate(swap_blocks((lane_f[0] < 0.5, lane_f[1] < 0.5), xs)):
-                        OUT[buf, dest[base + n], db * 16 : (db + 1) * 16, g * 128 : (g + 1) * 128] = v
-
-        def post_pair(s, j):
-            buf = s % 2
+            for v in range(lo, mid) if part == 0 else range(mid, hi):
+                for m in range(2):
+                    g, db = v // 2, 2 * m + v % 2
+                    f = pltpu.matmul_pop(wide[m][(3 * buf + c) % 2][v - lo])
+                    low, high = [], []
+                    for i4 in range(4):
+                        i = g * 4 + i4
+                        x = (f[i4 * 16 : (i4 + 1) * 16, :] * ANG[s, i : i + 1, :]).astype(BF)
+                        low.append(x[:, :128])
+                        high.append(x[:, 128:])
+                    for base, xs in ((0, low), (4, high)):
+                        for n, y in enumerate(swap_blocks((lane_f[0] < 0.5, lane_f[1] < 0.5), xs)):
+                            OUT[buf, dest[base + n], db * 16 : (db + 1) * 16, g * 128 : (g + 1) * 128] = y
+
+        def post_pair(s, buf, j):
             e, u = j // 4, (j // 2) % 2
             for m in range(2):
                 nt = u * 2 + m
@@ -400,45 +408,50 @@
                     v = f[:, h * 128 : (h + 1) * 128] * ANGP[s, e, g : g + 1, :]
                     OUT[buf, roles[s, 0, PAIR + e], :, g * 128 : (g + 1) * 128] = v.astype(BF)
 
-        def copy(s):
+        def copy(s, buf):
             place = (s % 4) * 4 + ((s // 4) % 2) * 2 + s // 8
-            return pltpu.make_async_copy(OUT.at[s % 2, pl.ds(0, CAP)], out.at[pl.ds(place * CAP, CAP)], sem.at[s % 2])
+            return pltpu.make_async_copy(OUT.at[buf, pl.ds(0, CAP)], out.at[pl.ds(place * CAP, CAP)], sem.at[buf])
 
         turn(0, 0)
         turn(0, 1)
-        push_wide(0)
+        push_wide(0, 0)
         push_pair(0, 0)
-        step(0, 0, 0)
-
-        def sender(s, _):
+        step(0, 0, 0, 0)
+
+        def sender(s, buf):
             nxt = jnp.minimum(s + 1, NS - 1)
             dest = [roles[s, 0, DEST + n] for n in range(CAP)]
 
             @pl.when(s >= 2)
             def _():
-                copy(s - 2).wait()
+                copy(s - 2, buf).wait()
 
             for k in range(1, len(STEPS) + 1):
                 if k < len(STEPS):
-                    step(s, k, nxt)
+                    step(s, buf, k, nxt)
                     what = STEPS[k]
                 else:
-                    step(nxt, 0, nxt)
-                    what = (6, 0)
+                    step(nxt, 1 - buf, 0, nxt)
+                    what = (len(CHUNKS), 0, 0)
                 if isinstance(what, int):
                     continue
                 done = STEPS[k - 1]
                 if isinstance(done, int) and done % 2 == 1 and k < len(STEPS):
-                    post_pair(s, done)
+                    post_pair(s, buf, done)
                 c = what[0]
                 if c > 0:
-                    first = not any(not isinstance(w, int) and w[0] == c for w in STEPS[:k])
-                    post_wide(s, c - 1, 0 if first else 1, dest)
-            post_wide(s, 5, 1, dest)
-            copy(s).start()
+                    n = sum(not isinstance(w, int) and w[0] == c for w in STEPS[:k])
+                    if n < 2:
+                        post_wide(s, buf, c - 1, n, dest)
+            post_wide(s, buf, len(CHUNKS) - 1, 1, dest)
+            copy(s, buf).start()
+
+        def two(t, _):
+            sender(2 * t, 0)
+            sender(2 * t + 1, 1)
             return 0
 
-        lax.fori_loop(0, NS, sender, 0)
+        lax.fori_loop(0, NS // 2, two, 0)
         left = jnp.zeros((64, 256), F32)
         for m in range(2):
             pltpu.matmul_acc_lhs(wide[m][0][0], kt_ref[:, halves(m)], load_staged_rhs=0)
@@ -446,8 +459,8 @@
             for acc in (*wide[m][0], narrow[m][0]):
                 left = left + pltpu.matmul_pop(acc)
         OUT[0, CAP, :, 0:256] = left.astype(BF)
-        copy(NS - 2).wait()
-        copy(NS - 1).wait()
+        copy(NS - 2, 0).wait()
+        copy(NS - 1, 1).wait()
 
     pl.run_scoped(whole, *[pltpu.ACC(m)((64, 256), F32) for m in range(2) for _ in range(16)])
 

time: 48.4 us -> 48 us (level)
  no operation moved by 1% of the time
where the time goes in v6:
time: 48 us; the launch traced here: 47.8 us
  Pallas kernels  47.8 us (100%)
    pallas_call x1, Pallas kernels, forms(): pl.pallas_call(forms_kernel, in_specs=[pl.BlockSpec(memory_space=pltpu.SM...  27 us
    pallas_call x1, Pallas kernels, gather(): pl.pallas_call(gather_kernel, in_specs=[pl.BlockSpec(memory_space=pltpu.H...  20.8 us

profile of v6, /device:TPU:1, one launch (start us, length us, event | category | flops | bytes accessed | tf_op | source)
XLA Modules:
  0.0 47.8 jit_solution(11023063907166684758)
XLA Ops:
  0.0 20.8 %shard_map.64 = (bf16[49,32,512]{2,1,0:T(8,128)(2,1)S(1)}, s32[16,1,128]{2,1,0:T(1,128)S(1)}, f32[16,32,256]{2,1,0:T(8,128)S(1)}, f32[16,2,8,128]{3,2,1,0:T(8,128)S(1)}, bf16[64,512]{1,0:T(8,128)(2,1)S(1)}) custom-call(bf16[64,96]{1,0:T(8,128)(2,1)} %bitcast.7, s32[1,96]{1,0:T(1,128)} %bitcast.8, s32[1,64]{1,0:T(1,128)} %bitcast.9, s32[1,64]{1,0:T(1,128)} %bitcast.10, ...), custom_call_target="tpu_custom_call" | custom-call | tf_op jit(solution)/shard_map/pallas_call | solution.py:473
  20.8 27.0 %shard_map.65 = bf16[128,64,1024]{2,1,0:T(8,128)(2,1)} custom-call(s32[16,1,128]{2,1,0:T(1,128)S(1)} %get-tuple-element.10.roles, bf16[49,32,512]{2,1,0:T(8,128)(2,1)S(1)} %get-tuple-element.11.W, f32[16,32,256]{2,1,0:T(8,128)S(1)} %get-tuple-element.12.ANG, f32[16,2,8,128]{3,2,1,0:T(8,128)S(1)} %get-tuple-element.13.ANGP, ...), custom_call_target="tpu_custom_call" | custom-call | tf_op jit(solution)/shard_map/pallas_call | solution.py:506
